TPU v7x, 128 devices: a whole 4x4x4 slice. The times are simulated.
128 devices in a mesh: pos: 64 (over y, x_hi, z, core), frame: 2 (over x_lo).
Axes of the slice: x: 4 (x_hi: 2, x_lo: 2; x = x_hi * 2 + x_lo), y: 4, z: 4, core: 2. Of those that a mesh axis runs over, the one named last changes fastest.
Arguments:
- tokens: bfloat16 [8, 16, 256, 768], P('frame', None, 'pos'), may hold values from -6 to 6
- modulation: float32 [8, 2, 2, 6, 768], P('frame'), may hold values from -3 to 3
- box_bounds: int32 [8, 6], P('frame'), may hold values from 0 to 16, as said below
- masters: float32 [896, 128, 128], P('pos')
- left_stats: float32 [896, 128, 128], P('pos'), as said below
- right_stats: float32 [896, 128, 128], P('pos'), as said below
- left_roots: float32 [896, 128, 128], P('pos'), as said below
- right_roots: float32 [896, 128, 128], P('pos'), as said below
- owner_slot: int32 [864], replicated, may hold values from 0 to 895, as said below
- cotangent: bfloat16 [8, 16, 256, 768], P('frame', None, 'pos'), may hold values from -6 to 6
Outputs:
- block_output: bfloat16 [8, 16, 256, 768], P('frame', None, 'pos')
- token_grads: bfloat16 [8, 16, 256, 768], P('frame', None, 'pos')
- tile_grads: float32 [896, 128, 128], P('pos')
- new_left: float32 [896, 128, 128], P('pos')
- new_right: float32 [896, 128, 128], P('pos')
- new_masters: float32 [896, 128, 128], P('pos')
Inputs may be any that keep to these rules, and one draw needn't show every extreme that they name: Distinct slots: tile t of the weights is held at slot owner_slot[t]; the other 32 slots hold no tile. For each clip c: box_bounds[c, 0] < box_bounds[c, 1] <= 16, box_bounds[c, 2] < box_bounds[c, 3] <= 16, box_bounds[c, 4] < box_bounds[c, 5] <= 16. `left_stats`: each slot's matrix is symmetric positive definite. `right_stats`: each slot's matrix is symmetric positive definite. `left_roots`: each slot's matrix is symmetric positive definite. `right_roots`: each slot's matrix is symmetric positive definite.
All inputs are finite; a program needn't handle non-finite values.
Results may differ from a plain program's by a relative error of at most 0.015.
Values may be sent and summed in bfloat16 or wider, within the bound.
No kernel may reach another device: no remote copies, remote signals or barrier semaphores. Data moves between devices by JAX's collectives and lax.ppermute only.
A program may use at most 320 MiB of HBM per device.

v0:
```python
import functools

import jax
import jax.numpy as jnp
from jax import lax
from jax.experimental import pallas as pl
from jax.experimental.pallas import tpu as pltpu
from jax.sharding import Mesh
from jax.sharding import PartitionSpec as P

D = 768
HEADS = 12
HD = 64
FF = 3072
GRID = 16
BLOCK = 128
TOK = 256
CH = 256
POS = ("pos_0", "pos_1", "pos_2", "pos_3")
EVERY = ("pos_0", "pos_1", "pos_2", "pos_3", "frame")

highest = lax.Precision.HIGHEST
stat_decay = 0.5
learning_rate = 0.7
norm_epsilon = 1e-06
f32 = jnp.float32
bf16 = jnp.bfloat16

QKV_AT, OUT_AT, FIRST_AT, SECOND_AT, LAYER_TILES = 0, 108, 144, 288, 432


def dot_nn(a, b):
    return lax.dot_general(a, b, (((1,), (0,)), ((), ())), preferred_element_type=f32)


def dot_nt(a, b):
    return lax.dot_general(a, b, (((1,), (1,)), ((), ())), preferred_element_type=f32)


def dot_tn(a, b):
    return lax.dot_general(a, b, (((0,), (0,)), ((), ())), preferred_element_type=f32)


def side(parts):
    return jnp.concatenate(parts, axis=1)


def norm_parts(values):
    center = values - jnp.mean(values, axis=-1, keepdims=True)
    spread = jnp.mean(center * center, axis=-1, keepdims=True)
    inverse = lax.rsqrt(spread + norm_epsilon)
    return center * inverse, inverse


def norm_back(normal, inverse, grad):
    return inverse * (
        grad
        - jnp.mean(grad, axis=-1, keepdims=True)
        - normal * jnp.mean(grad * normal, axis=-1, keepdims=True)
    )


def fill_mask(mask_ref, box_ref, clips):
    span = TOK // clips
    ids = lax.broadcasted_iota(jnp.int32, (span, BLOCK), 0)
    for clip in range(clips):
        low_f, high_f, low_r, high_r, low_c, high_c = (box_ref[6 * clip + k] for k in range(6))
        base = box_ref[6 * clips]
        frames = jnp.full((span, BLOCK), base, jnp.int32) if clips == 1 else ids >> 2
        patches = ids if clips == 1 else base + (ids & 3)
        rows, cols = patches >> 4, patches & 15
        within = (low_f <= frames) & (frames < high_f) & (low_r <= rows) & (rows < high_r) & (low_c <= cols) & (cols < high_c)
        mask_ref[clip * span : (clip + 1) * span, :] = jnp.where(within, 1.0, 0.0)


def picked_row(mod_ref, mask_ref, row):
    clips = mod_ref.shape[0]
    span = TOK // clips
    parts = []
    for clip in range(clips):
        inside_box = side([mask_ref[clip * span : (clip + 1) * span, :]] * (D // BLOCK)) > 0.5
        parts.append(
            jnp.where(
                inside_box,
                jnp.broadcast_to(mod_ref[clip, 1, row : row + 1, :], (span, D)),
                jnp.broadcast_to(mod_ref[clip, 0, row : row + 1, :], (span, D)),
            )
        )
    return parts[0] if clips == 1 else jnp.concatenate(parts, axis=0)


def fetch(slots_refs, where_ref, held, sem, base, row_tiles, col_tiles):
    step = 6

    def one(turn, carry):
        col = turn // (row_tiles // step)
        first = (turn % (row_tiles // step)) * step
        for k in range(step):
            row = first + k
            target = held.at[col, pl.ds(pl.multiple_of(row * BLOCK, BLOCK), BLOCK), :]
            place = where_ref[base + row * col_tiles + col]
            for ref, start, end in ((slots_refs[0], 0, 64 * BY_GATHER), (slots_refs[1], 64 * BY_GATHER, 64 * 14)):

                @pl.when(jnp.logical_and(place >= start, place < end))
                def _(ref=ref, start=start):
                    pltpu.make_async_copy(ref.at[place - start], target, sem).start()

        return carry

    lax.fori_loop(0, col_tiles * (row_tiles // step), one, 0)


def fetch_done(held, sem):
    pltpu.make_async_copy(held, held, sem).wait()


def forward_part(x, mod_ref, mask_ref, weights, waits, kept, same):
    wq, wo, w1, w2 = weights
    qkv_s, probs_s, attended_s, slope_s, active_s = kept
    lane = lax.broadcasted_iota(jnp.int32, (TOK, BLOCK), 1)
    low_half = lane < HD

    normal, _ = norm_parts(x)
    normed = (normal * (1.0 + picked_row(mod_ref, mask_ref, 1)) + picked_row(mod_ref, mask_ref, 0)).astype(bf16)
    waits[0]()

    def project(j, carry):
        qkv_s[j] = dot_nn(normed, side([wq[2 * j], wq[2 * j + 1]])).astype(bf16)
        return carry

    lax.fori_loop(0, 9, project, 0, unroll=True)

    def attend(c, carry):
        for pair in range(2):
            cols = slice(pair * BLOCK, (pair + 1) * BLOCK)
            q, k, v = qkv_s[c, :, cols], qkv_s[3 + c, :, cols], qkv_s[6 + c, :, cols]
            outs = []
            for e in range(2):
                mine = low_half if e == 0 else jnp.logical_not(low_half)
                scores = dot_nt(k, jnp.where(mine, q, jnp.zeros_like(q))) * HD ** (-0.5)
                if same is not None:
                    scores = jnp.where(same, scores, -jnp.inf)
                grown = jnp.exp(scores - jnp.max(scores, axis=0, keepdims=True))
                probs = (grown * (1.0 / jnp.sum(grown, axis=0, keepdims=True))).astype(bf16)
                probs_s[4 * c + 2 * pair + e] = probs
                outs.append(dot_tn(probs, v))
            attended_s[c, :, cols] = jnp.where(low_half, outs[0], outs[1]).astype(bf16)
        return carry

    lax.fori_loop(0, 3, attend, 0, unroll=True)
    attended = side([attended_s[c] for c in range(3)])
    waits[1]()
    branch = side([dot_nn(attended, side([wo[2 * j], wo[2 * j + 1]])) for j in range(3)])
    middle = x + picked_row(mod_ref, mask_ref, 2) * branch
    normal, _ = norm_parts(middle)
    renormed = (normal * (1.0 + picked_row(mod_ref, mask_ref, 4)) + picked_row(mod_ref, mask_ref, 3)).astype(bf16)
    waits[2]()

    def widen(j, carry):
        u = dot_nn(renormed, side([w1[2 * j], w1[2 * j + 1]]))
        root = (2.0 / 3.141592653589793) ** 0.5
        square = u * u
        bent = jnp.tanh(root * (u + 0.044715 * (square * u)))
        active_s[j] = (0.5 * u * (1.0 + bent)).astype(bf16)
        slope_s[j] = (
            0.5 * (1.0 + bent) + 0.5 * u * (1.0 - bent * bent) * (root * (1.0 + 3 * 0.044715 * square))
        ).astype(bf16)
        return carry

    lax.fori_loop(0, 12, widen, 0, unroll=True)
    active = side([active_s[j] for j in range(12)])
    waits[3]()
    mlp = side([dot_nn(active, side([w2[2 * j], w2[2 * j + 1]])) for j in range(3)])
    return middle, renormed, middle + picked_row(mod_ref, mask_ref, 5) * mlp


def send_tile(tile_ref, place, grads_refs, sem):
    start = 0
    for ref in grads_refs:
        size = ref.shape[0]

        @pl.when(jnp.logical_and(place >= start, place < start + size))
        def _(ref=ref, start=start):
            pltpu.make_async_copy(tile_ref, ref.at[place - start], sem).start()

        start += size


def send_tiles(stage, grads_refs, place_ref, sem, at, col_tiles, value, row, col):
    rows, cols = value.shape[0] // BLOCK, value.shape[1] // BLOCK
    for j in range(cols):
        for i in range(rows):
            tile = at + (row + i) * col_tiles + (col + j)
            stage[tile] = value[i * BLOCK : (i + 1) * BLOCK, j * BLOCK : (j + 1) * BLOCK].astype(bf16)
            send_tile(stage.at[tile], place_ref[tile], grads_refs, sem)


def backward_part(x, middle, renormed, upstream, mod_ref, mask_ref, weights, waits, kept, stage, grads_refs, place_ref, sem, acc, wide_s):
    wq, wo, w1, w2 = weights
    qkv_s, probs_s, attended_s, slope_s, active_s = kept
    lane = lax.broadcasted_iota(jnp.int32, (TOK, BLOCK), 1)
    low_half = lane < HD
    send = functools.partial(send_tiles, stage, grads_refs, place_ref, sem)

    grad_mlp = (picked_row(mod_ref, mask_ref, 5) * upstream).astype(bf16)
    renormed_t = renormed.T
    acc[...] = jnp.zeros_like(acc)
    waits[3]()
    waits[2]()

    def narrow(j, carry):
        rows = pl.ds(pl.multiple_of(j * CH, CH), CH)
        grad_active = dot_nt(grad_mlp, side([w2[n, rows, :] for n in range(6)]))
        grad_hidden = (grad_active * slope_s[j].astype(f32)).astype(bf16)
        acc[...] += dot_nt(grad_hidden, side([w1[2 * j], w1[2 * j + 1]]))
        send(FIRST_AT, 24, dot_nn(renormed_t, grad_hidden), 0, 2 * j)
        send(SECOND_AT, 6, dot_tn(active_s[j], grad_mlp), 2 * j, 0)
        return carry

    lax.fori_loop(0, 12, narrow, 0, unroll=True)
    normal, inverse = norm_parts(middle)
    grad_middle = upstream + norm_back(normal, inverse, (1.0 + picked_row(mod_ref, mask_ref, 4)) * acc[...])
    grad_branch = (picked_row(mod_ref, mask_ref, 2) * grad_middle).astype(bf16)
    waits[1]()

    def attend(c, carry):
        rows = pl.ds(pl.multiple_of(c * CH, CH), CH)
        grad_attended = dot_nt(grad_branch, side([wo[n, rows, :] for n in range(6)])).astype(bf16)
        send(OUT_AT, 6, dot_tn(attended_s[c], grad_branch), 2 * c, 0)
        for pair in range(2):
            cols = slice(pair * BLOCK, (pair + 1) * BLOCK)
            q, k, v = qkv_s[c, :, cols], qkv_s[3 + c, :, cols], qkv_s[6 + c, :, cols]
            ga = grad_attended[:, cols]
            grads = []
            for e in range(2):
                mine = low_half if e == 0 else jnp.logical_not(low_half)
                probs_low = probs_s[4 * c + 2 * pair + e]
                probs = probs_low.astype(f32)
                weighed = probs * dot_nt(v, jnp.where(mine, ga, jnp.zeros_like(ga)))
                grad_scores = (weighed - probs * jnp.sum(weighed, axis=0, keepdims=True)).astype(bf16)
                grads.append((dot_tn(grad_scores, k), dot_nn(grad_scores, q), dot_nn(probs_low, ga)))
            for n, scaling in ((0, HD ** (-0.5)), (1, HD ** (-0.5)), (2, 1.0)):
                wide_s[3 * n + c, :, cols] = (
                    jnp.where(low_half, grads[0][n], grads[1][n]) * scaling
                ).astype(bf16)
        return carry

    lax.fori_loop(0, 3, attend, 0, unroll=True)
    normal, inverse = norm_parts(x)
    scale_one = 1.0 + picked_row(mod_ref, mask_ref, 1)
    normed_t = (normal * scale_one + picked_row(mod_ref, mask_ref, 0)).astype(bf16).T
    acc[...] = jnp.zeros_like(acc)
    waits[0]()

    def gather_in(j, carry):
        piece = wide_s[j]
        acc[...] += dot_nt(piece, side([wq[2 * j], wq[2 * j + 1]]))
        send(QKV_AT, 18, dot_nn(normed_t, piece), 0, 2 * j)
        return carry

    lax.fori_loop(0, 9, gather_in, 0, unroll=True)
    normal, inverse = norm_parts(x)
    return grad_middle + norm_back(normal, inverse, scale_one * acc[...])


def same_sequence():
    rows = lax.broadcasted_iota(jnp.int32, (TOK, TOK), 0)
    cols = lax.broadcasted_iota(jnp.int32, (TOK, TOK), 1)
    return jnp.logical_and(rows // 64 == cols // 64, rows % 4 == cols % 4)


WEIGHT_SCRATCH = [
    pltpu.VMEM((18, D, BLOCK), bf16),
    pltpu.VMEM((6, D, BLOCK), bf16),
    pltpu.VMEM((24, D, BLOCK), bf16),
    pltpu.VMEM((6, FF, BLOCK), bf16),
    pltpu.SemaphoreType.DMA((4,)),
]
KEPT = [
    ((9, TOK, CH), bf16),
    ((HEADS, TOK, TOK), bf16),
    ((3, TOK, CH), bf16),
    ((12, TOK, CH), bf16),
    ((12, TOK, CH), bf16),
]
WEIGHT_RUNS = ((QKV_AT, 6, 18), (OUT_AT, 6, 6), (FIRST_AT, 6, 24), (SECOND_AT, 24, 6))


def fetch_all(slots_refs, where_ref, held, sems, base, order):
    for n in order:
        at, rows, cols = WEIGHT_RUNS[n]
        fetch(slots_refs, where_ref, held[n], sems.at[n], base + at, rows, cols)
    return [functools.partial(fetch_done, held[n], sems.at[n]) for n in range(4)]


def first_forward(where_ref, box_ref, x_ref, mods_ref, gathered_ref, passed_ref, middle_ref, out_ref, *rest):
    mask_ref, rest = rest[-1], rest[:-1]
    fill_mask(mask_ref, box_ref, 1)
    mod_ref = mods_ref.at[pl.ds(box_ref[7], 1), 0]
    kept, (wq, wo, w1, w2, sems) = rest[:5], rest[5:]
    weights = (wq, wo, w1, w2)
    waits = fetch_all((gathered_ref, passed_ref), where_ref, weights, sems, 0, (0, 1, 2, 3))
    middle, _, output = forward_part(x_ref[...].astype(f32), mod_ref, mask_ref, weights, waits, kept, None)
    middle_ref[...] = middle
    out_ref[...] = output.astype(bf16)


def second_layer(
    where_ref, place_ref, box_ref, x_ref, up_ref, mods_ref, gathered_ref, passed_ref, out_ref, grad_ref, *rest
):
    mask_ref, rest = rest[-1], rest[:-1]
    fill_mask(mask_ref, box_ref, 4)
    mod_ref = mods_ref.at[:, 1]
    grads_refs, rest = rest[:6], rest[6:]
    kept, (wq, wo, w1, w2, sems, stage, sem, acc, wide_s) = rest[:5], rest[5:]
    weights = (wq, wo, w1, w2)
    waits = fetch_all((gathered_ref, passed_ref), where_ref, weights, sems, LAYER_TILES, (0, 1, 2, 3))
    x = x_ref[...].astype(f32)
    middle, renormed, output = forward_part(x, mod_ref, mask_ref, weights, waits, kept, same_sequence())
    out_ref[...] = output.astype(bf16)
    nothing = [lambda: None] * 4
    grad = backward_part(
        x, middle, renormed, up_ref[...].astype(f32), mod_ref, mask_ref, weights, nothing, kept,
        stage, grads_refs, place_ref.at[pl.ds(LAYER_TILES, LAYER_TILES)], sem, acc, wide_s,
    )
    grad_ref[...] = grad.astype(bf16)
    pltpu.make_async_copy(stage, stage, sem).wait()


def first_backward(
    where_ref, place_ref, box_ref, x_ref, middle_ref, up_ref, mods_ref, gathered_ref, passed_ref,
    qkv_s, probs_s, attended_s, slope_s, active_s, *rest,
):
    mask_ref, rest = rest[-1], rest[:-1]
    fill_mask(mask_ref, box_ref, 1)
    mod_ref = mods_ref.at[pl.ds(box_ref[7], 1), 0]
    grad_ref, *grads_refs = rest[6:13]
    wq, wo, w1, w2, sems, stage, sem, acc, wide_s = rest[13:]
    weights = (wq, wo, w1, w2)
    waits = fetch_all((gathered_ref, passed_ref), where_ref, weights, sems, 0, (3, 2, 1, 0))
    x, middle = x_ref[...].astype(f32), middle_ref[...]
    normal, _inverse = norm_parts(middle)
    renormed = (normal * (1.0 + picked_row(mod_ref, mask_ref, 4)) + picked_row(mod_ref, mask_ref, 3)).astype(bf16)
    grad = backward_part(
        x, middle, renormed, up_ref[...].astype(f32), mod_ref, mask_ref, weights, waits,
        (qkv_s, probs_s, attended_s, slope_s, active_s), stage, grads_refs, place_ref, sem, acc, wide_s,
    )
    grad_ref[...] = grad.astype(bf16)
    pltpu.make_async_copy(stage, stage, sem).wait()


SMEM = pl.BlockSpec(memory_space=pltpu.SMEM)
VMEM = pl.BlockSpec(memory_space=pltpu.VMEM)
ANY = pl.BlockSpec(memory_space=pl.ANY)
MASK = pltpu.VMEM((TOK, BLOCK), f32)
PARAMS = pltpu.CompilerParams(vmem_limit_bytes=60 * 1024 * 1024)
BACK_SCRATCH = [
    pltpu.VMEM((LAYER_TILES, BLOCK, BLOCK), bf16),
    pltpu.SemaphoreType.DMA,
    pltpu.VMEM((TOK, D), f32),
    pltpu.VMEM((9, TOK, CH), bf16),
]


PARTS = (140, 112, 196)
GRADS = [jax.ShapeDtypeStruct((n, BLOCK, BLOCK), bf16) for n in PARTS + PARTS]


def run_first_forward(where, box, x, mods, slots):
    return pl.pallas_call(
        first_forward,
        name="first_forward",
        out_shape=[jax.ShapeDtypeStruct((TOK, D), f32), jax.ShapeDtypeStruct((TOK, D), bf16)]
        + [jax.ShapeDtypeStruct(s, t) for s, t in KEPT],
        in_specs=[SMEM, SMEM, VMEM, VMEM, ANY, ANY],
        out_specs=[VMEM] * 7,
        scratch_shapes=WEIGHT_SCRATCH + [MASK],
        compiler_params=PARAMS,
    )(where, box, x, mods, *slots)


def run_second(where, place, box, x, up, mods, slots):
    return pl.pallas_call(
        second_layer,
        name="second_layer",
        out_shape=[
            jax.ShapeDtypeStruct((TOK, D), bf16),
            jax.ShapeDtypeStruct((TOK, D), bf16),
            *GRADS,
        ],
        in_specs=[SMEM, SMEM, SMEM, VMEM, VMEM, VMEM, ANY, ANY],
        out_specs=[VMEM, VMEM] + [ANY] * 6,
        scratch_shapes=[pltpu.VMEM(s, t) for s, t in KEPT] + WEIGHT_SCRATCH + BACK_SCRATCH + [MASK],
        compiler_params=PARAMS,
    )(where, place, box, x, up, mods, *slots)


def run_first_backward(where, place, box, x, middle, up, mods, slots, kept, grads):
    return pl.pallas_call(
        first_backward,
        name="first_backward",
        out_shape=[
            jax.ShapeDtypeStruct((TOK, D), bf16),
            *GRADS,
        ],
        in_specs=[SMEM] * 3 + [VMEM] * 4 + [ANY] * 2 + [VMEM] * 5 + [ANY] * 6,
        out_specs=[VMEM] + [ANY] * 6,
        scratch_shapes=WEIGHT_SCRATCH + BACK_SCRATCH + [MASK],
        input_output_aliases={14 + k: 1 + k for k in range(6)},
        compiler_params=PARAMS,
    )(where, place, box, x, middle, up, mods, *slots, *kept, *grads)


def everyone():
    for y in range(4):
        for xh in range(2):
            for z in range(4):
                for c in range(2):
                    for xl in range(2):
                        yield (y, xh, z, c, xl)


def number(y, xh, z, c, xl):
    return (((y * 2 + xh) * 4 + z) * 2 + c) * 2 + xl


def permute(value, target):
    return lax.ppermute(value, EVERY, [(number(*d), number(*target(*d))) for d in everyone()])


def along(axis, step):
    def target(y, xh, z, c, xl):
        if (axis == 0) == (c == 0):
            return ((y + step) % 4, xh, z, c, xl)
        return (y, xh, (z + step) % 4, c, xl)

    return target


def other_core(y, xh, z, c, xl):
    return (y, xh, z, 1 - c, xl)


def across(y, xh, z, c, xl):
    return (y, 1 - xh, z, c, 1 - xl)


def twin(y, xh, z, c, xl):
    return (y, xh, z, c, 1 - xl)


def added(*values):
    total = values[0].astype(f32)
    for value in values[1:]:
        total = total + value.astype(f32)
    return total.astype(bf16)


def pair(y, xh, z, c, xl):
    return twin(y, xh, z, c, xl) if c == 0 else across(y, xh, z, c, xl)


def opposite(y, xh, z, c, xl):
    return (y, 1 - xh, z, c, xl)


def pair_last(y, xh, z, c, xl):
    return across(y, xh, z, c, xl) if c == 0 else twin(y, xh, z, c, xl)


PIECES = {
    "plain2": (0, 56), "given2": (56, 28), "given13": (84, 56), "plain13": (140, 112), "kept2": (252, 28),
    "kept13": (280, 56), "given0": (336, 28), "kept0": (364, 28), "plain0": (392, 56),
}
TILE_STEP = 7


def add_tiles(plan, source_count, last_count, *refs):
    sources, outs = refs[:source_count], refs[source_count + last_count :]
    for out, parts in zip(outs, plan):
        for at, size, terms in parts:
            step = TILE_STEP if size % TILE_STEP == 0 else size

            def some(i, carry, out=out, at=at, terms=terms, step=step):
                for k in range(step):
                    n = i * step + k
                    total = sources[terms[0][0]][terms[0][1] + n].astype(f32)
                    for source, start in terms[1:]:
                        total = total + sources[source][start + n].astype(f32)
                    out[at + n] = total.astype(bf16)
                return carry

            lax.fori_loop(0, size // step, some, 0)


def keep(*refs):
    pass


FREE = pl.CostEstimate(flops=1, bytes_accessed=1, transcendentals=0)


class TileSums:
    def __init__(self):
        self.last = []

    def __call__(self, plan, *sources, after=()):
        sizes = [sum(size for _, size, _ in parts) for parts in plan]
        last = [*self.last, *after]
        tiles = sum(sizes) + sum(value.shape[0] for value in sources)
        outs = pl.pallas_call(
            functools.partial(add_tiles, plan, len(sources), len(last)),
            name="add_tiles",
            out_shape=[jax.ShapeDtypeStruct((n, BLOCK, BLOCK), bf16) for n in sizes]
            + [jax.ShapeDtypeStruct((8, BLOCK), f32)],
            in_specs=[VMEM] * len(sources) + [ANY] * len(last),
            out_specs=[VMEM] * len(sizes) + [ANY],
            compiler_params=pltpu.CompilerParams(vmem_limit_bytes=tiles * 32768 + 1024 * 1024),
            cost_estimate=FREE,
        )(*sources, *last)
        self.last = [outs[-1]]
        return outs[:-1]


def then(value, *last):
    return pl.pallas_call(
        keep,
        name="keep",
        out_shape=jax.ShapeDtypeStruct(value.shape, value.dtype),
        in_specs=[ANY] * (1 + len(last)),
        out_specs=ANY,
        input_output_aliases={0: 0},
        cost_estimate=FREE,
    )(value, *last)


def reduce_tiles(mine, given, core, frame, token_blocks, send_tokens, renew):
    add = TileSums()
    at = {name: start for name, (start, _) in PIECES.items()}

    def alone(size, *terms):
        return [(0, size, list(terms))]

    got = permute(given[0], other_core)
    p2_a, p2_b, over = add(
        [alone(28, (0, 0), (1, 0)), alone(28, (0, 28), (1, 28)), alone(84, (0, 56), (1, 56))], mine[0], got
    )
    p2_ahead, p2_behind = permute(p2_a, along(0, 1)), permute(p2_b, along(0, -1))
    x213 = permute(over, pair)
    got = permute(then(given[1], *add.last), other_core)
    last_got = permute(then(given[2], *add.last), other_core)
    p13 = add(
        [
            [(0, 28, [(0, 0), (1, 0), (2, 0)]), (28, 28, [(0, 28), (1, 28)])],
            [(0, 28, [(0, 56), (1, 56)]), (28, 28, [(0, 84), (1, 84), (3, 0)])],
        ],
        mine[1], got, p2_ahead, p2_behind,
    )
    p1, p3 = permute(p13[0], along(0, 1)), permute(p13[1], along(0, -1))
    mine, got = mine[2], last_got
    at = {name: start - 252 for name, start in at.items()}
    x0 = permute(add([alone(28, (0, at["given0"]), (1, at["given0"]))], mine, got)[0], pair)
    h2 = add([alone(14, (0, at["kept2"] + n), (1, at["kept2"] + n), (2, n)) for n in (0, 14)], mine, got, x213)
    h2_ahead, h2_behind = permute(h2[0], along(0, 1)), permute(h2[1], along(0, -1))

    def split(start, cuts):
        return [
            alone(size, (0, start + n), (1, start + n), *((k, n) for k in more)) for n, size, more in cuts
        ]

    p = add(
        split(at["plain0"], [(28, 7, (2, 3)), (35, 7, (2, 3)), (0, 14, (2, 3)), (14, 14, (2, 3)), (42, 14, (2, 3))]),
        mine, got, p1, p3,
    )
    ahead, behind = permute(p[0], along(1, 1)), permute(p[1], along(1, -1))
    k13 = r13 = at["kept13"]
    h13 = add(
        [
            [(0, 14, [(0, k13), (1, r13), (2, 28), (3, 0)]), (14, 14, [(0, k13 + 14), (1, r13 + 14), (2, 42)])],
            [(0, 14, [(0, k13 + 28), (1, r13 + 28), (2, 56)]), (14, 14, [(0, k13 + 42), (1, r13 + 42), (2, 70), (4, 0)])],
        ],
        mine, got, x213, h2_ahead, h2_behind,
    )
    h1, h3 = permute(h13[0], along(0, 1)), permute(h13[1], along(0, -1))
    sides = add(
        [
            [(0, 7, [(0, 0), (1, 0)]), (7, 7, [(0, 7)])],
            [(0, 7, [(2, 0)]), (7, 7, [(2, 7), (3, 0)])],
        ],
        p[3], ahead, p[4], behind,
    )
    up, down = permute(sides[0], along(1, 1)), permute(sides[1], along(1, -1))
    h = add(
        split(at["kept0"], [(14, 4, (2, 3, 4)), (18, 3, (2, 3, 4)), (0, 7, (2, 3, 4)), (7, 7, (2, 3, 4)), (21, 7, (2, 3, 4))]),
        mine, got, x0, h1, h3,
    )
    h_ahead, h_behind = permute(h[0], along(1, 1)), permute(h[1], along(1, -1))
    token_blocks = send_tokens(then(token_blocks, *add.last))
    p = add([alone(7, (0, n), (1, n), (2, n)) for n in (0, 7)], p[2], up, down)
    far = permute(p[1], across)
    sides = add(
        [
            [(0, 4, [(0, 0), (1, 0)]), (4, 3, [(0, 4)])],
            [(0, 4, [(2, 0)]), (4, 3, [(2, 4), (3, 0)])],
        ],
        h[3], h_ahead, h[4], h_behind,
    )
    h_up, h_down = permute(sides[0], along(1, 1)), permute(sides[1], along(1, -1))
    (p,) = add([alone(7, (0, 0), (1, 0))], p[0], far)
    match = permute(p, twin)
    (h,) = add([alone(7, (0, 0), (1, 0), (2, 0))], h[2], h_up, h_down, after=[token_blocks])
    beyond, beside, around = permute(h, pair_last), permute(h, twin), permute(h, opposite)
    told = (core == 0) & (frame == 1)
    h = added(jnp.where(told, beside, h), jnp.where(told, around, beyond))
    renewed = renew([p, match])
    return renewed, permute(then(h, renewed[0]), other_core), token_blocks


def precondition(term_count, info_ref, *refs):
    terms, refs = refs[:term_count], refs[term_count:]
    sources, refs = refs[:5], refs[-14:]
    outs, held, made, sems = refs[:4], refs[4:9], refs[9:13], refs[13]
    start = info_ref[0]
    loads = [
        pltpu.make_async_copy(source.at[pl.ds(start, 7)], here, sems.at[n])
        for n, (source, here) in enumerate(zip(sources, held))
    ]
    for load in loads:
        load.start()
    for load in loads:
        load.wait()
    masters, left_stats, right_stats, left_roots, right_roots = held
    grads, new_left, new_right, new_masters = made

    def product(a, b, dims):
        return lax.dot_general(a, b, (dims, ((), ())), preferred_element_type=f32, precision=highest)

    for n in range(7):
        total = terms[0][n].astype(f32)
        for term in terms[1:]:
            total = total + term[n].astype(f32)
        grad = jnp.where(info_ref[1 + start + n] > 0, total, 0.0)
        grads[n] = grad
        new_left[n] = stat_decay * left_stats[n] + (1.0 - stat_decay) * product(grad, grad, ((1,), (1,)))
        new_right[n] = stat_decay * right_stats[n] + (1.0 - stat_decay) * product(grad, grad, ((0,), (0,)))
        rotated = product(grad, right_roots[n], ((1,), (0,)))
        new_masters[n] = masters[n] - learning_rate * product(left_roots[n], rotated, ((1,), (0,)))
    stores = [
        pltpu.make_async_copy(here, out.at[pl.ds(start, 7)], sems.at[n]) for n, (here, out) in enumerate(zip(made, outs))
    ]
    for store in stores:
        store.start()
    for store in stores:
        store.wait()


def run_precondition(info, terms, sources, outs):
    seven = pltpu.VMEM((7, BLOCK, BLOCK), f32)
    return pl.pallas_call(
        functools.partial(precondition, len(terms)),
        name="precondition",
        out_shape=[jax.ShapeDtypeStruct((14, BLOCK, BLOCK), f32)] * 4,
        in_specs=[SMEM] + [VMEM] * len(terms) + [ANY] * (5 + len(outs)),
        out_specs=[ANY] * 4,
        scratch_shapes=[seven] * 9 + [pltpu.SemaphoreType.DMA((5,))],
        input_output_aliases={6 + len(terms) + k: k for k in range(len(outs))},
        compiler_params=pltpu.CompilerParams(vmem_limit_bytes=16 * 1024 * 1024),
        cost_estimate=pl.CostEstimate(flops=7 * 4 * 6 * 2 * BLOCK**3, bytes_accessed=7 * 9 * 65536, transcendentals=0),
    )(info, *terms, *sources, *outs)


BY_GATHER = 7
OTHERS = 14 - BY_GATHER


def gather_tiles(tiles, beside):
    gathered = lax.all_gather(tiles[:BY_GATHER], POS, axis=0, tiled=True)
    here, n = tiles[BY_GATHER:], OTHERS
    base = jnp.concatenate([here, permute(here, across)], axis=0)
    behind, ahead = permute(base, along(1, 1)), permute(base, along(1, -1))
    far = [permute(behind[:n], along(1, 1)), permute(ahead[n:], along(1, -1))]
    own = jnp.concatenate([base, behind, ahead, *far], axis=0)
    behind, ahead = permute(own, along(0, 1)), permute(own, along(0, -1))
    far = [permute(behind[: 4 * n], along(0, 1)), permute(ahead[4 * n :], along(0, -1))]
    near = jnp.concatenate([own, behind, ahead], axis=0)
    far = then(jnp.concatenate(far, axis=0), *beside)
    passed = jnp.concatenate([near, far, permute(near, other_core), permute(far, other_core)], axis=0)
    return gathered, passed


def source_of(slots, y, xh, z, core):
    owner, k = slots // 14, slots % 14
    owner_y, owner_xh, owner_z, owner_c = owner // 16, owner // 8 % 2, owner // 2 % 4, owner % 2
    ahead_y, ahead_z = (owner_y - y) % 4, (owner_z - z) % 4
    first = jnp.where(owner_c == 0, ahead_y, ahead_z)
    second = jnp.where(owner_c == 0, ahead_z, ahead_y)

    def rank(ring):
        return jnp.where(ring == 3, 1, jnp.where(ring == 1, 2, jnp.where(ring == 2, 3, 0)))

    place = (((owner_c + core) % 2 * 4 + rank(first)) * 4 + rank(second)) * 2 + (owner_xh + xh) % 2
    place = 64 * BY_GATHER + place * OTHERS + k - BY_GATHER
    return jnp.where(k < BY_GATHER, owner * BY_GATHER + k, place).astype(jnp.int32)


def place_of(slots, y, xh, z, core, frame):
    owner, k = slots // 14, slots % 14
    owner_y, owner_xh, owner_z, owner_c = owner // 16, owner // 8 % 2, owner // 2 % 4, owner % 2
    handler = k // 7
    ahead_y, ahead_z = (owner_y - y) % 4, (owner_z - z) % 4
    first = jnp.where(handler == 0, ahead_y, ahead_z)
    second = jnp.where(handler == 0, ahead_z, ahead_y)
    over_x = (owner_xh + xh) % 2
    kept = jnp.where(handler == 0, (over_x + frame) % 2, over_x) == 0

    def start(prefix, size):
        at0, at2, at13 = (PIECES[prefix + ring][0] for ring in ("0", "2", "13"))
        return jnp.where(first == 0, at0, jnp.where(first == 2, at2, at13 + size * (first // 2)))

    plain = start("plain", 56) + (second * 2 + over_x) * 7
    halved = jnp.where(kept, start("kept", 28), start("given", 28)) + second * 7
    place = jnp.where(owner_c == handler, plain, halved) + k % 7
    return ((handler + core) % 2 * 448 + place).astype(jnp.int32)


def local(
    tokens,
    modulation,
    box_bounds,
    masters,
    left_stats,
    right_stats,
    left_roots,
    right_roots,
    owner_slot,
    cotangent,
):
    y, xh, z, core = (lax.axis_index(a) for a in POS)
    mine, copy = lax.axis_index(POS), lax.axis_index("frame")

    def to_frames(value):
        return lax.all_to_all(value.reshape(64, 4, D), POS, 0, 0, tiled=True).reshape(TOK, D)

    clip, frame = mine // 16, mine % 16
    bounds_here = lax.dynamic_index_in_dim(box_bounds, clip, 0, keepdims=False)
    box_first = jnp.concatenate([bounds_here, jnp.stack([frame, clip])]).astype(jnp.int32)
    box_second = jnp.concatenate([box_bounds.reshape(24), jnp.stack([mine * 4])]).astype(jnp.int32)
    where = source_of(owner_slot, y, xh, z, core)
    place = place_of(owner_slot, y, xh, z, core, copy)
    upstream = cotangent.reshape(TOK, D)
    tokens_here = to_frames(tokens)
    slots = gather_tiles(masters.astype(bf16), [tokens_here, where, place])
    middle, passed, *kept = run_first_forward(where, box_first, tokens_here, modulation, slots)
    here = to_frames(passed)
    block_output, grad_here, *grads = run_second(where, place, box_second, here, upstream, modulation, slots)
    upstream = to_frames(grad_here)
    token_grads, *grads = run_first_backward(
        where, place, box_first, tokens_here, middle, upstream, modulation, slots, kept, grads
    )
    slot_ids = mine * 14 + jnp.arange(14, dtype=jnp.int32)
    holds = jnp.any(owner_slot[None, :] == slot_ids[:, None], axis=1)
    sources = [masters, left_stats, right_stats, left_roots, right_roots]

    def info(start):
        return jnp.concatenate([jnp.stack([start]), holds]).astype(jnp.int32)

    def renew(terms):
        return run_precondition(info(core * 7), terms, sources, [])

    renewed, halved, token_grads = reduce_tiles(grads[:3], grads[3:], core, copy, token_grads, to_frames, renew)
    renewed = run_precondition(info(7 - core * 7), [halved], sources, renewed)
    return (block_output.reshape(tokens.shape), token_grads.reshape(tokens.shape), *renewed)


def solution(mesh):
    split = Mesh(
        mesh.devices.reshape(4, 2, 4, 2, mesh.shape["frame"]),
        ("pos_0", "pos_1", "pos_2", "pos_3", "frame"),
    )
    return jax.shard_map(
        local,
        mesh=split,
        in_specs=(
            P("frame", None, POS, None),
            P("frame", None, None, None, None),
            P("frame", None),
            P(POS, None, None),
            P(POS, None, None),
            P(POS, None, None),
            P(POS, None, None),
            P(POS, None, None),
            P(),
            P("frame", None, POS, None),
        ),
        out_specs=(
            P("frame", None, POS, None),
            P("frame", None, POS, None),
            P(POS, None, None),
            P(POS, None, None),
            P(POS, None, None),
            P(POS, None, None),
        ),
        check_vma=False,
    )
```

profile of v0, /device:TPU:1, one launch (start us, length us, event | category | flops | bytes accessed | tf_op | source)
XLA Modules:
  0.0 390.4 jit_solution(7342499203972396587)
XLA Ops:
  9.5 3.4 collective-permute-start
  12.9 4.9 %collective-permute-done = bf16[7,128,128]{2,1,0:T(8,128)(2,1)S(1)} collective-permute-done((bf16[7,128,128]{2,1,0:T(8,128)(2,1)S(1)}, bf16[7,128,128]{2,1,0:T(8,128)(2,1)S(1)}, u32[]{:S(2)}, u32[]{:S(2)}) %collective-permute-start) | collective-permute-done | bytes 229408 | tf_op jit(solution)/shard_map/ppermute | solution.py:428
  17.9 3.1 collective-permute-start.2
  21.9 4.5 %collective-permute-done.2 = bf16[14,128,128]{2,1,0:T(8,128)(2,1)S(1)} collective-permute-done((bf16[14,128,128]{2,1,0:T(8,128)(2,1)S(1)}, bf16[14,128,128]{2,1,0:T(8,128)(2,1)S(1)}, u32[]{:S(2)}, u32[]{:S(2)}) %collective-permute-start.2) | collective-permute-done | bytes 458784 | tf_op jit(solution)/shard_map/ppermute | solution.py:428
  26.4 3.2 collective-permute-start.4
  32.5 4.4 %collective-permute-done.3 = bf16[7,128,128]{2,1,0:T(8,128)(2,1)S(1)} collective-permute-done((bf16[7,128,128]{2,1,0:T(8,128)(2,1)S(1)}, bf16[7,128,128]{2,1,0:T(8,128)(2,1)S(1)}, u32[]{:S(2)}, u32[]{:S(2)}) %collective-permute-start.3) | collective-permute-done | bytes 229408 | tf_op jit(solution)/shard_map/ppermute | solution.py:428
  38.8 2.8 collective-permute-start.5
  43.9 30.5 %collective-permute-done.5 = bf16[56,128,128]{2,1,0:T(8,128)(2,1)S(1)} collective-permute-done((bf16[56,128,128]{2,1,0:T(8,128)(2,1)S(1)}, bf16[56,128,128]{2,1,0:T(8,128)(2,1)S(1)}, u32[]{:S(2)}, u32[]{:S(2)}) %collective-permute-start.5) | collective-permute-done | bytes 1835040 | tf_op jit(solution)/shard_map/ppermute | solution.py:428
  74.4 2.7 constant_dynamic-update-slice_fusion.7
  77.1 2.8 constant_dynamic-update-slice_fusion.6
  82.9 7.1 %all-to-all-start = ((bf16[64,4,768]{2,1,0:T(4,128)(2,1)}), bf16[64,4,768]{2,1,0:T(4,128)(2,1)S(1)}, u32[]{:S(2)}, u32[]{:S(2)}) async-start(bf16[64,4,768]{2,1,0:T(4,128)(2,1)} %bitcast.4), calls=%async_computation | async-start | bytes 786432 | tf_op jit(solution)/shard_map/all_to_all | solution.py:742
  90.7 16.3 %all-to-all-done = bf16[64,4,768]{2,1,0:T(4,128)(2,1)S(1)} async-done(((bf16[64,4,768]{2,1,0:T(4,128)(2,1)}), bf16[64,4,768]{2,1,0:T(4,128)(2,1)S(1)}, u32[]{:S(2)}, u32[]{:S(2)}) %all-to-all-start) | async-done | bytes 393248 | tf_op jit(solution)/shard_map/all_to_all | solution.py:742
  111.2 3.0 constant_dynamic-update-slice_fusion.16
  114.2 7.4 %constant_dynamic-update-slice_fusion.15 = bf16[448,128,128]{2,1,0:T(8,128)(2,1)} fusion(bf16[448,128,128]{2,1,0:T(8,128)(2,1)} %constant_dynamic-update-slice_fusion.16, bf16[168,128,128]{2,1,0:T(8,128)(2,1)} %collective-permute-done.9), kind=kLoop, calls=%fused_computation.19 | loop fusion | bytes 11010048
  123.0 14.5 %first_forward.1 = (f32[256,768]{1,0:T(8,128)}, bf16[256,768]{1,0:T(8,128)(2,1)}, bf16[9,256,256]{2,1,0:T(8,128)(2,1)}, bf16[12,256,256]{2,1,0:T(8,128)(2,1)}, b...) custom-call(s32[864]{0:T(1024)} %get-tuple-element.169.refs_2_.where_ref, ...), custom_call_target="tpu_custom_call" | custom-call | tf_op jit(solution)/shard_map/first_forward/pallas_call | solution.py:370
  139.3 5.3 %all-to-all-start.1 = ((bf16[64,4,768]{2,1,0:T(4,128)(2,1)}), bf16[64,4,768]{2,1,0:T(4,128)(2,1)S(1)}, u32[]{:S(2)}, u32[]{:S(2)}) async-start(bf16[64,4,768]{2,1,0:T(4,128)(2,1)} %reshape.53), calls=%async_computation.1 | async-start | bytes 786432 | tf_op jit(solution)/shard_map/all_to_all | solution.py:742
  146.2 11.1 %all-to-all-done.1 = bf16[64,4,768]{2,1,0:T(4,128)(2,1)S(1)} async-done(((bf16[64,4,768]{2,1,0:T(4,128)(2,1)}), bf16[64,4,768]{2,1,0:T(4,128)(2,1)S(1)}, u32[]{:S(2)}, u32[]{:S(2)}) %all-to-all-start.1) | async-done | bytes 393248 | tf_op jit(solution)/shard_map/all_to_all | solution.py:742
  158.1 28.3 %second_layer.1 = (bf16[256,768]{1,0:T(8,128)(2,1)}, bf16[256,768]{1,0:T(8,128)(2,1)}, bf16[140,128,128]{2,1,0:T(8,128)(2,1)}, bf16[112,128,128]{2,1,0:T(8,128)(...) custom-call(s32[864]{0:T(1024)} %get-tuple-element.169.refs_2_.where, ...), custom_call_target="tpu_custom_call" | custom-call | tf_op jit(solution)/shard_map/second_layer/pallas_call | solution.py:383
  187.5 17.0 %all_to_all.20 = bf16[64,4,768]{2,1,0:T(4,128)(2,1)S(1)} all-to-all(bf16[64,4,768]{2,1,0:T(4,128)(2,1)S(1)} %reshape.57), channel_id=1, replica_groups=mesh['pos_0'=4,'pos_1'=2,'pos_2'=4,'pos_3'=2,'frame'=2] {'pos_0','pos_1'..., dimensions={0} | all-to-all | bytes 786432 | tf_op jit(solution)/shard_map/all_to_all | solution.py:742
  205.4 23.6 %first_backward.1 = (bf16[256,768]{1,0:T(8,128)(2,1)}, bf16[140,128,128]{2,1,0:T(8,128)(2,1)}, bf16[112,128,128]{2,1,0:T(8,128)(2,1)}, bf16[196,128,128]{2,1,0:T...) custom-call(s32[864]{0:T(1024)} %get-tuple-element.169.refs_2_.where, ...), custom_call_target="tpu_custom_call", output_to_operand_aliasing={{1}: (14, {}), {2}: (15, {}), {3}: (16, {}), {4}: (17, {}),... | custom-call | tf_op jit(solution)/shard_map/first_backward/pallas_call | solution.py:399
  229.5 7.6 %collective-permute-done.11.refs_1_ = bf16[140,128,128]{2,1,0:T(8,128)(2,1)S(1)} collective-permute-done((bf16[140,128,128]{2,1,0:T(8,128)(2,1)}, bf16[140,128,128]{2,1,0:T(8,128)(2,1)S(1)}, u32[]{:S(2)}, u32[]{:S(2)}) %collective-permute-start.11) | collective-permute-done | bytes 4587552 | tf_op jit(solution)/shard_map/ppermute | solution.py:428
  247.5 11.3 %collective-permute-done.14.refs_2_ = bf16[28,128,128]{2,1,0:T(8,128)(2,1)S(1)} collective-permute-done((bf16[28,128,128]{2,1,0:T(8,128)(2,1)}, bf16[28,128,128]{2,1,0:T(8,128)(2,1)S(1)}, u32[]{:S(2)}, u32[]{:S(2)}) %collective-permute-start.14) | collective-permute-done | bytes 917536 | tf_op jit(solution)/shard_map/ppermute | solution.py:428
  265.3 3.0 add_tiles.14
  268.3 9.4 %collective-permute-done.17.refs_2_ = bf16[84,128,128]{2,1,0:T(8,128)(2,1)S(1)} collective-permute-done((bf16[84,128,128]{2,1,0:T(8,128)(2,1)}, bf16[84,128,128]{2,1,0:T(8,128)(2,1)S(1)}, u32[]{:S(2)}, u32[]{:S(2)}) %collective-permute-start.17) | collective-permute-done | bytes 2752544 | tf_op jit(solution)/shard_map/ppermute | solution.py:428
  277.8 3.2 add_tiles.15
  286.2 3.7 add_tiles.16
  291.1 3.7 add_tiles.17
  300.2 6.0 %collective-permute-done.24.refs_1_ = bf16[7,128,128]{2,1,0:T(8,128)(2,1)S(1)} collective-permute-done((bf16[7,128,128]{2,1,0:T(8,128)(2,1)S(1)}, bf16[7,128,128]{2,1,0:T(8,128)(2,1)S(1)}, u32[]{:S(2)}, u32[]{:S(2)}) %collective-permute-start.24) | collective-permute-done | bytes 229408 | tf_op jit(solution)/shard_map/ppermute | solution.py:428
  311.0 3.4 add_tiles.19
  319.0 12.2 %all-to-all-start.3 = ((bf16[64,4,768]{2,1,0:T(4,128)(2,1)}), bf16[64,4,768]{2,1,0:T(4,128)(2,1)}, u32[]{:S(2)}, u32[]{:S(2)}) async-start(bf16[64,4,768]{2,1,0:T(4,128)(2,1)} %reshape.59), calls=%async_computation.3 | async-start | bytes 786432 | tf_op jit(solution)/shard_map/all_to_all | solution.py:742
  358.2 6.6 %precondition.2 = (f32[14,128,128]{2,1,0:T(8,128)}, f32[14,128,128]{2,1,0:T(8,128)}, f32[14,128,128]{2,1,0:T(8,128)}, f32[14,128,128]{2,1,0:T(8,128)}) custom-call(s32[15]{0:T(128)S(1)} %get-tuple-element.170.info_ref, bf16[7,128,128]{2,1,0:T(8,128)(2,1)} %get-tuple-element.135.refs_0_, bf16[7,128,128]{2,1,0:T(8,128)(2,1)} %collective-permute-done.36.refs_1_, ...), custom_call_target="tpu_custom_call" | custom-call | flops 704643072 | bytes 4128768 | tf_op jit(solution)/shard_map/precondition/pallas_call | solution.py:659
  375.2 6.0 %precondition.3 = (f32[14,128,128]{2,1,0:T(8,128)}, f32[14,128,128]{2,1,0:T(8,128)}, f32[14,128,128]{2,1,0:T(8,128)}, f32[14,128,128]{2,1,0:T(8,128)}) custom-call(s32[15]{0:T(128)S(1)} %get-tuple-element.171.info_ref, ...), custom_call_target="tpu_custom_call", output_to_operand_aliasing={{0}: (7, {}), {1}: (8, {}), {2}: (9, {}), {3}: (10, {})} | custom-call | flops 704643072 | bytes 4128768 | tf_op jit(solution)/shard_map/precondition/pallas_call | solution.py:659
  (174 shorter events, 103.7 us)
Async XLA Ops:
  7.2 115.9 %all-gather.2.cloned.1.call-start = ((), (), s32[]{:S(2)}) async-start(), calls=%async_computation.4 | async-start | bytes 14909440 | tf_op jit(solution)/shard_map/all_gather | solution.py:677
  21.0 8.8 %collective-permute-start.1 = (bf16[14,128,128]{2,1,0:T(8,128)(2,1)S(1)}, bf16[14,128,128]{2,1,0:T(8,128)(2,1)S(1)}, u32[]{:S(2)}, u32[]{:S(2)}) collective-permute-start(bf16[14,128,128]{2,1,0:T(8,128)(2,1)S(1)} %pad_maximum_fusion.1), channel_id=1, source_target_pairs={{0,4},{1,5},{2,34},{3,35},{4,8},{5,9},{6,38},{7,39},{8,12},{9,13},... | collective-permute-start | bytes 1376264 | tf_op jit(solution)/shard_map/ppermute | solution.py:428
  26.4 11.4 %collective-permute-start.4 = (bf16[7,128,128]{2,1,0:T(8,128)(2,1)S(1)}, bf16[7,128,128]{2,1,0:T(8,128)(2,1)S(1)}, u32[]{:S(2)}, u32[]{:S(2)}) collective-permute-start(bf16[7,128,128]{2,1,0:T(8,128)(2,1)S(1)} %slice.27), channel_id=1, source_target_pairs={{0,12},{1,13},{2,98},{3,99},{4,0},{5,1},{6,102},{7,103},{8,4},{9,5... | collective-permute-start | bytes 688136 | tf_op jit(solution)/shard_map/ppermute | solution.py:428
  38.8 35.5 %collective-permute-start.5 = (bf16[56,128,128]{2,1,0:T(8,128)(2,1)S(1)}, bf16[56,128,128]{2,1,0:T(8,128)(2,1)S(1)}, u32[]{:S(2)}, u32[]{:S(2)}) collective-permute-start(bf16[56,128,128]{2,1,0:T(8,128)(2,1)S(1)} %get-tuple-element.161), channel_id=1, source_target_pairs={{0,32},{1,33},{2,6},{3,7},{4,36},{5,37},{6,10},{7,11},{8,40},{9,41... | collective-permute-start | bytes 5505032 | tf_op jit(solution)/shard_map/ppermute | solution.py:428
  41.6 35.5 %collective-permute-start.6 = (bf16[56,128,128]{2,1,0:T(8,128)(2,1)S(1)}, bf16[56,128,128]{2,1,0:T(8,128)(2,1)S(1)}, u32[]{:S(2)}, u32[]{:S(2)}) collective-permute-start(bf16[56,128,128]{2,1,0:T(8,128)(2,1)S(1)} %get-tuple-element.161), channel_id=1, source_target_pairs={{0,96},{1,97},{2,14},{3,15},{4,100},{5,101},{6,2},{7,3},{8,104},{9... | collective-permute-start | bytes 5505032 | tf_op jit(solution)/shard_map/ppermute | solution.py:428
  79.9 34.3 %collective-permute-start.9 = (bf16[168,128,128]{2,1,0:T(8,128)(2,1)}, bf16[168,128,128]{2,1,0:T(8,128)(2,1)}, u32[]{:S(2)}, u32[]{:S(2)}) collective-permute-start(bf16[168,128,128]{2,1,0:T(8,128)(2,1)} %get-tuple-element.144), channel_id=1, source_target_pairs={{0,2},{1,3},{2,0},{3,1},{4,6},{5,7},{6,4},{7,5},{8,10},{9,11},{10,... | collective-permute-start | bytes 16515080 | tf_op jit(solution)/shard_map/ppermute | solution.py:428
  79.9 27.9 %collective-permute-start.8 = (bf16[28,128,128]{2,1,0:T(8,128)(2,1)S(1)}, bf16[28,128,128]{2,1,0:T(8,128)(2,1)S(1)}, u32[]{:S(2)}, u32[]{:S(2)}) collective-permute-start(bf16[28,128,128]{2,1,0:T(8,128)(2,1)S(1)} %slice.29), channel_id=1, source_target_pairs={{0,96},{1,97},{2,14},{3,15},{4,100},{5,101},{6,2},{7,3},{8,104},{9... | collective-permute-start | bytes 2752520 | tf_op jit(solution)/shard_map/ppermute | solution.py:428
  82.9 24.9 %collective-permute-start.7 = (bf16[28,128,128]{2,1,0:T(8,128)(2,1)}, bf16[28,128,128]{2,1,0:T(8,128)(2,1)S(1)}, u32[]{:S(2)}, u32[]{:S(2)}) collective-permute-start(bf16[28,128,128]{2,1,0:T(8,128)(2,1)} %slice.28), channel_id=1, source_target_pairs={{0,32},{1,33},{2,6},{3,7},{4,36},{5,37},{6,10},{7,11},{8,40},{9,41... | collective-permute-start | bytes 2752520 | tf_op jit(solution)/shard_map/ppermute | solution.py:428
  82.9 24.0 %all-to-all-start = ((bf16[64,4,768]{2,1,0:T(4,128)(2,1)}), bf16[64,4,768]{2,1,0:T(4,128)(2,1)S(1)}, u32[]{:S(2)}, u32[]{:S(2)}) async-start(bf16[64,4,768]{2,1,0:T(4,128)(2,1)} %bitcast.4), calls=%async_computation | async-start | bytes 786432 | tf_op jit(solution)/shard_map/all_to_all | solution.py:742
  109.2 12.4 %collective-permute-start.10 = (bf16[56,128,128]{2,1,0:T(8,128)(2,1)}, bf16[56,128,128]{2,1,0:T(8,128)(2,1)S(1)}, u32[]{:S(2)}, u32[]{:S(2)}) collective-permute-start(bf16[56,128,128]{2,1,0:T(8,128)(2,1)} %keep.5), channel_id=1, source_target_pairs={{0,2},{1,3},{2,0},{3,1},{4,6},{5,7},{6,4},{7,5},{8,10},{9,11},{10,... | collective-permute-start | bytes 5505032 | tf_op jit(solution)/shard_map/ppermute | solution.py:428
  139.3 17.9 %all-to-all-start.1 = ((bf16[64,4,768]{2,1,0:T(4,128)(2,1)}), bf16[64,4,768]{2,1,0:T(4,128)(2,1)S(1)}, u32[]{:S(2)}, u32[]{:S(2)}) async-start(bf16[64,4,768]{2,1,0:T(4,128)(2,1)} %reshape.53), calls=%async_computation.1 | async-start | bytes 786432 | tf_op jit(solution)/shard_map/all_to_all | solution.py:742
  243.6 21.6 %collective-permute-start.12 = (bf16[196,128,128]{2,1,0:T(8,128)(2,1)}, bf16[196,128,128]{2,1,0:T(8,128)(2,1)}, u32[]{:S(2)}, u32[]{:S(2)}) collective-permute-start(bf16[196,128,128]{2,1,0:T(8,128)(2,1)} %keep.6), channel_id=1, source_target_pairs={{0,2},{1,3},{2,0},{3,1},{4,6},{5,7},{6,4},{7,5},{8,10},{9,11},{10,... | collective-permute-start | bytes 19267592 | tf_op jit(solution)/shard_map/ppermute | solution.py:428
  244.0 15.3 %collective-permute-start.13 = (bf16[112,128,128]{2,1,0:T(8,128)(2,1)}, bf16[112,128,128]{2,1,0:T(8,128)(2,1)S(1)}, u32[]{:S(2)}, u32[]{:S(2)}) collective-permute-start(bf16[112,128,128]{2,1,0:T(8,128)(2,1)} %keep.7), channel_id=1, source_target_pairs={{0,2},{1,3},{2,0},{3,1},{4,6},{5,7},{6,4},{7,5},{8,10},{9,11},{10,... | collective-permute-start | bytes 11010056 | tf_op jit(solution)/shard_map/ppermute | solution.py:428
  244.1 33.6 %collective-permute-start.17 = (bf16[84,128,128]{2,1,0:T(8,128)(2,1)}, bf16[84,128,128]{2,1,0:T(8,128)(2,1)S(1)}, u32[]{:S(2)}, u32[]{:S(2)}) collective-permute-start(bf16[84,128,128]{2,1,0:T(8,128)(2,1)} %copy-done.19), channel_id=1, source_target_pairs={{0,1},{1,0},{2,19},{3,18},{4,5},{5,4},{6,23},{7,22},{8,9},{9,8},{1... | collective-permute-start | bytes 8257544 | tf_op jit(solution)/shard_map/ppermute | solution.py:428
  244.8 14.0 %collective-permute-start.14 = (bf16[28,128,128]{2,1,0:T(8,128)(2,1)}, bf16[28,128,128]{2,1,0:T(8,128)(2,1)S(1)}, u32[]{:S(2)}, u32[]{:S(2)}) collective-permute-start(bf16[28,128,128]{2,1,0:T(8,128)(2,1)} %copy-done.20), channel_id=1, source_target_pairs={{0,32},{1,33},{2,6},{3,7},{4,36},{5,37},{6,10},{7,11},{8,40},{9,41... | collective-permute-start | bytes 2752520 | tf_op jit(solution)/shard_map/ppermute | solution.py:428
  245.2 13.6 %collective-permute-start.15 = (bf16[28,128,128]{2,1,0:T(8,128)(2,1)S(1)}, bf16[28,128,128]{2,1,0:T(8,128)(2,1)S(1)}, u32[]{:S(2)}, u32[]{:S(2)}) collective-permute-start(bf16[28,128,128]{2,1,0:T(8,128)(2,1)S(1)} %get-tuple-element.99), channel_id=1, source_target_pairs={{0,96},{1,97},{2,14},{3,15},{4,100},{5,101},{6,2},{7,3},{8,104},{9... | collective-permute-start | bytes 2752520 | tf_op jit(solution)/shard_map/ppermute | solution.py:428
  262.5 23.6 %collective-permute-start.20 = (bf16[56,128,128]{2,1,0:T(8,128)(2,1)S(1)}, bf16[56,128,128]{2,1,0:T(8,128)(2,1)S(1)}, u32[]{:S(2)}, u32[]{:S(2)}) collective-permute-start(bf16[56,128,128]{2,1,0:T(8,128)(2,1)S(1)} %get-tuple-element.106), channel_id=1, source_target_pairs={{0,32},{1,33},{2,6},{3,7},{4,36},{5,37},{6,10},{7,11},{8,40},{9,41... | collective-permute-start | bytes 5505032 | tf_op jit(solution)/shard_map/ppermute | solution.py:428
  263.0 23.2 %collective-permute-start.21 = (bf16[56,128,128]{2,1,0:T(8,128)(2,1)S(1)}, bf16[56,128,128]{2,1,0:T(8,128)(2,1)S(1)}, u32[]{:S(2)}, u32[]{:S(2)}) collective-permute-start(bf16[56,128,128]{2,1,0:T(8,128)(2,1)S(1)} %get-tuple-element.107), channel_id=1, source_target_pairs={{0,96},{1,97},{2,14},{3,15},{4,100},{5,101},{6,2},{7,3},{8,104},{9... | collective-permute-start | bytes 5505032 | tf_op jit(solution)/shard_map/ppermute | solution.py:428
  280.9 10.1 %collective-permute-start.18 = (bf16[14,128,128]{2,1,0:T(8,128)(2,1)S(1)}, bf16[14,128,128]{2,1,0:T(8,128)(2,1)S(1)}, u32[]{:S(2)}, u32[]{:S(2)}) collective-permute-start(bf16[14,128,128]{2,1,0:T(8,128)(2,1)S(1)} %get-tuple-element.104), channel_id=1, source_target_pairs={{0,32},{1,33},{2,6},{3,7},{4,36},{5,37},{6,10},{7,11},{8,40},{9,41... | collective-permute-start | bytes 1376264 | tf_op jit(solution)/shard_map/ppermute | solution.py:428
  281.4 9.7 %collective-permute-start.19 = (bf16[14,128,128]{2,1,0:T(8,128)(2,1)S(1)}, bf16[14,128,128]{2,1,0:T(8,128)(2,1)S(1)}, u32[]{:S(2)}, u32[]{:S(2)}) collective-permute-start(bf16[14,128,128]{2,1,0:T(8,128)(2,1)S(1)} %get-tuple-element.105), channel_id=1, source_target_pairs={{0,96},{1,97},{2,14},{3,15},{4,100},{5,101},{6,2},{7,3},{8,104},{9... | collective-permute-start | bytes 1376264 | tf_op jit(solution)/shard_map/ppermute | solution.py:428
  283.7 26.2 %collective-permute-start.16 = (bf16[28,128,128]{2,1,0:T(8,128)(2,1)S(1)}, bf16[28,128,128]{2,1,0:T(8,128)(2,1)S(1)}, u32[]{:S(2)}, u32[]{:S(2)}) collective-permute-start(bf16[28,128,128]{2,1,0:T(8,128)(2,1)S(1)} %get-tuple-element.101), channel_id=1, source_target_pairs={{0,1},{1,0},{2,19},{3,18},{4,5},{5,4},{6,23},{7,22},{8,9},{9,8},{1... | collective-permute-start | bytes 2752520 | tf_op jit(solution)/shard_map/ppermute | solution.py:428
  294.7 16.3 %collective-permute-start.22 = (bf16[28,128,128]{2,1,0:T(8,128)(2,1)S(1)}, bf16[28,128,128]{2,1,0:T(8,128)(2,1)S(1)}, u32[]{:S(2)}, u32[]{:S(2)}) collective-permute-start(bf16[28,128,128]{2,1,0:T(8,128)(2,1)S(1)} %get-tuple-element.110), channel_id=1, source_target_pairs={{0,32},{1,33},{2,6},{3,7},{4,36},{5,37},{6,10},{7,11},{8,40},{9,41... | collective-permute-start | bytes 2752520 | tf_op jit(solution)/shard_map/ppermute | solution.py:428
  294.8 16.2 %collective-permute-start.23 = (bf16[28,128,128]{2,1,0:T(8,128)(2,1)S(1)}, bf16[28,128,128]{2,1,0:T(8,128)(2,1)S(1)}, u32[]{:S(2)}, u32[]{:S(2)}) collective-permute-start(bf16[28,128,128]{2,1,0:T(8,128)(2,1)S(1)} %get-tuple-element.111), channel_id=1, source_target_pairs={{0,96},{1,97},{2,14},{3,15},{4,100},{5,101},{6,2},{7,3},{8,104},{9... | collective-permute-start | bytes 2752520 | tf_op jit(solution)/shard_map/ppermute | solution.py:428
  297.5 8.6 %collective-permute-start.24 = (bf16[7,128,128]{2,1,0:T(8,128)(2,1)S(1)}, bf16[7,128,128]{2,1,0:T(8,128)(2,1)S(1)}, u32[]{:S(2)}, u32[]{:S(2)}) collective-permute-start(bf16[7,128,128]{2,1,0:T(8,128)(2,1)S(1)} %get-tuple-element.113), channel_id=1, source_target_pairs={{0,4},{1,5},{2,34},{3,35},{4,8},{5,9},{6,38},{7,39},{8,12},{9,13},... | collective-permute-start | bytes 688136 | tf_op jit(solution)/shard_map/ppermute | solution.py:428
  307.2 25.8 %collective-permute-start.28 = (bf16[14,128,128]{2,1,0:T(8,128)(2,1)}, bf16[14,128,128]{2,1,0:T(8,128)(2,1)}, u32[]{:S(2)}, u32[]{:S(2)}) collective-permute-start(bf16[14,128,128]{2,1,0:T(8,128)(2,1)} %get-tuple-element.125), channel_id=1, source_target_pairs={{0,4},{1,5},{2,34},{3,35},{4,8},{5,9},{6,38},{7,39},{8,12},{9,13},... | collective-permute-start | bytes 1376264 | tf_op jit(solution)/shard_map/ppermute | solution.py:428
  307.2 25.8 %collective-permute-start.29 = (bf16[14,128,128]{2,1,0:T(8,128)(2,1)}, bf16[14,128,128]{2,1,0:T(8,128)(2,1)}, u32[]{:S(2)}, u32[]{:S(2)}) collective-permute-start(bf16[14,128,128]{2,1,0:T(8,128)(2,1)} %get-tuple-element.126), channel_id=1, source_target_pairs={{0,12},{1,13},{2,98},{3,99},{4,0},{5,1},{6,102},{7,103},{8,4},{9,5... | collective-permute-start | bytes 1376264 | tf_op jit(solution)/shard_map/ppermute | solution.py:428
  319.0 30.6 %all-to-all-start.3 = ((bf16[64,4,768]{2,1,0:T(4,128)(2,1)}), bf16[64,4,768]{2,1,0:T(4,128)(2,1)}, u32[]{:S(2)}, u32[]{:S(2)}) async-start(bf16[64,4,768]{2,1,0:T(4,128)(2,1)} %reshape.59), calls=%async_computation.3 | async-start | bytes 786432 | tf_op jit(solution)/shard_map/all_to_all | solution.py:742
  331.2 10.5 %collective-permute-start.26 = (bf16[4,128,128]{2,1,0:T(8,128)(2,1)}, bf16[4,128,128]{2,1,0:T(8,128)(2,1)S(1)}, u32[]{:S(2)}, u32[]{:S(2)}) collective-permute-start(bf16[4,128,128]{2,1,0:T(8,128)(2,1)} %copy-done.21), channel_id=1, source_target_pairs={{0,4},{1,5},{2,34},{3,35},{4,8},{5,9},{6,38},{7,39},{8,12},{9,13},... | collective-permute-start | bytes 393224 | tf_op jit(solution)/shard_map/ppermute | solution.py:428
  336.2 10.8 %collective-permute-start.32 = (bf16[7,128,128]{2,1,0:T(8,128)(2,1)}, bf16[7,128,128]{2,1,0:T(8,128)(2,1)S(1)}, u32[]{:S(2)}, u32[]{:S(2)}) collective-permute-start(bf16[7,128,128]{2,1,0:T(8,128)(2,1)} %get-tuple-element.131), channel_id=1, source_target_pairs={{0,17},{1,16},{2,19},{3,18},{4,21},{5,20},{6,23},{7,22},{8,25},{9,... | collective-permute-start | bytes 688136 | tf_op jit(solution)/shard_map/ppermute | solution.py:428
  353.1 11.7 %collective-permute-start.35 = (bf16[7,128,128]{2,1,0:T(8,128)(2,1)}, bf16[7,128,128]{2,1,0:T(8,128)(2,1)S(1)}, u32[]{:S(2)}, u32[]{:S(2)}) collective-permute-start(bf16[7,128,128]{2,1,0:T(8,128)(2,1)} %get-tuple-element.134), channel_id=1, source_target_pairs={{0,17},{1,16},{2,3},{3,2},{4,21},{5,20},{6,7},{7,6},{8,25},{9,24},... | collective-permute-start | bytes 688136 | tf_op jit(solution)/shard_map/ppermute | solution.py:428
  353.7 11.1 %collective-permute-start.34 = (bf16[7,128,128]{2,1,0:T(8,128)(2,1)}, bf16[7,128,128]{2,1,0:T(8,128)(2,1)}, u32[]{:S(2)}, u32[]{:S(2)}) collective-permute-start(bf16[7,128,128]{2,1,0:T(8,128)(2,1)} %get-tuple-element.134), channel_id=1, source_target_pairs={{0,16},{1,17},{2,18},{3,19},{4,20},{5,21},{6,22},{7,23},{8,24},{9,... | collective-permute-start | bytes 688136 | tf_op jit(solution)/shard_map/ppermute | solution.py:428
  355.1 12.3 %collective-permute-start.33 = (bf16[7,128,128]{2,1,0:T(8,128)(2,1)}, bf16[7,128,128]{2,1,0:T(8,128)(2,1)}, u32[]{:S(2)}, u32[]{:S(2)}) collective-permute-start(bf16[7,128,128]{2,1,0:T(8,128)(2,1)} %get-tuple-element.134), channel_id=1, source_target_pairs={{0,1},{1,0},{2,3},{3,2},{4,5},{5,4},{6,7},{7,6},{8,9},{9,8},{10,11... | collective-permute-start | bytes 688136 | tf_op jit(solution)/shard_map/ppermute | solution.py:428
  (39 other events, 348.7 us)
Sparse Core Ops, SparseCore 0:
  11.8 109.2 all-gather.1
where the time goes:
time: 397 us; the launch traced here: 390 us
  waiting for transfers between devices  117 us (29%)
  Pallas kernels  105 us (26%)
  starting transfers between devices  73.6 us (19%)
  local copies, waits for them, and re-layouts  56.7 us (14%)
  blocking collectives  17 us (4%)
  between operations  14.8 us (4%)
  other arithmetic  6.65 us (2%)
    ppermute x38, waiting for transfers between devices, permute(): lax.ppermute(value, EVERY, [(number(*d), number(*target(*d))) for d in ev...  89.4 us
    ppermute x38, starting transfers between devices, permute(): lax.ppermute(value, EVERY, [(number(*d), number(*target(*d))) for d in ev...  49 us
    unnamed x69, local copies, waits for them, and re-layouts  41.2 us
    pallas_call x1, Pallas kernels, run_second(): pl.pallas_call(second_layer, name='second_layer', out_shape=[jax.ShapeDty...  28.3 us
    all_to_all x3, waiting for transfers between devices, to_frames(): lax.all_to_all(value.reshape(64, 4, D), POS, 0, 0, tiled=True)  27.4 us
    pallas_call x12, Pallas kernels, __call__(): pl.pallas_call(functools.partial(add_tiles, plan, len(sources), len(last)...  25.8 us
    all_to_all x3, starting transfers between devices, to_frames(): lax.all_to_all(value.reshape(64, 4, D), POS, 0, 0, tiled=True)  24.5 us
    pallas_call x1, Pallas kernels, run_first_backward(): pl.pallas_call(first_backward, name='first_backward', out_shape=[jax.Shap...  23.6 us
  transfers between devices with their start and end apart: 42, of which 20 were waited for; matrix products, arithmetic and copies ran while one was open for 9% of the time, Pallas kernels for 8%

commit v1 on v0

--- a/solution.py
+++ b/solution.py
@@ -513,8 +513,8 @@
             name="add_tiles",
             out_shape=[jax.ShapeDtypeStruct((n, BLOCK, BLOCK), bf16) for n in sizes]
             + [jax.ShapeDtypeStruct((8, BLOCK), f32)],
-            in_specs=[VMEM] * len(sources) + [ANY] * len(last),
-            out_specs=[VMEM] * len(sizes) + [ANY],
+            in_specs=[VMEM] * (len(sources) + len(self.last)) + [ANY] * len(after),
+            out_specs=[VMEM] * (len(sizes) + 1),
             compiler_params=pltpu.CompilerParams(vmem_limit_bytes=tiles * 32768 + 1024 * 1024),
             cost_estimate=FREE,
         )(*sources, *last)
@@ -664,7 +664,7 @@
         out_specs=[ANY] * 4,
         scratch_shapes=[seven] * 9 + [pltpu.SemaphoreType.DMA((5,))],
         input_output_aliases={6 + len(terms) + k: k for k in range(len(outs))},
-        compiler_params=pltpu.CompilerParams(vmem_limit_bytes=16 * 1024 * 1024),
+        compiler_params=pltpu.CompilerParams(vmem_limit_bytes=58 * 1024 * 1024),
         cost_estimate=pl.CostEstimate(flops=7 * 4 * 6 * 2 * BLOCK**3, bytes_accessed=7 * 9 * 65536, transcendentals=0),
     )(info, *terms, *sources, *outs)
 

time: 397 us -> 392 us (0.987)
  local copies, waits for them, and re-layouts: 56.7 us -> 52.6 us
    unnamed x69 -> x55, local copies, waits for them, and re-layouts: 41.2 us -> 36.1 us
  transfers between devices with their start and end apart: 42 -> 42, of which waited for: 20 -> 19; matrix products, arithmetic and copies ran while one was open for 9% -> 9% of each run, Pallas kernels for 8% -> 7%
where the time goes in v1:
time: 392 us; the launch traced here: 385 us
  waiting for transfers between devices  119 us (30%)
  Pallas kernels  102 us (26%)
  starting transfers between devices  73.5 us (19%)
  local copies, waits for them, and re-layouts  52.6 us (13%)
  blocking collectives  17 us (4%)
  between operations  14.8 us (4%)
  other arithmetic  6.23 us (2%)
    ppermute x38, waiting for transfers between devices, permute(): lax.ppermute(value, EVERY, [(number(*d), number(*target(*d))) for d in ev...  91.6 us
    ppermute x38, starting transfers between devices, permute(): lax.ppermute(value, EVERY, [(number(*d), number(*target(*d))) for d in ev...  48.9 us
    unnamed x55, local copies, waits for them, and re-layouts  36.1 us
    pallas_call x1, Pallas kernels, run_second(): pl.pallas_call(second_layer, name='second_layer', out_shape=[jax.ShapeDty...  28.3 us
    all_to_all x3, waiting for transfers between devices, to_frames(): lax.all_to_all(value.reshape(64, 4, D), POS, 0, 0, tiled=True)  27.4 us
    all_to_all x3, starting transfers between devices, to_frames(): lax.all_to_all(value.reshape(64, 4, D), POS, 0, 0, tiled=True)  24.6 us
    pallas_call x1, Pallas kernels, run_first_backward(): pl.pallas_call(first_backward, name='first_backward', out_shape=[jax.Shap...  23.6 us
    pallas_call x12, Pallas kernels, __call__(): pl.pallas_call(functools.partial(add_tiles, plan, len(sources), len(last)...  22.2 us
  transfers between devices with their start and end apart: 42, of which 19 were waited for; matrix products, arithmetic and copies ran while one was open for 9% of the time, Pallas kernels for 7%

profile of v1, /device:TPU:1, one launch (start us, length us, event | category | flops | bytes accessed | tf_op | source)
XLA Modules:
  0.0 385.2 jit_solution(16484778342976421824)
XLA Ops:
  9.5 3.4 collective-permute-start
  12.9 4.9 %collective-permute-done = bf16[7,128,128]{2,1,0:T(8,128)(2,1)S(1)} collective-permute-done((bf16[7,128,128]{2,1,0:T(8,128)(2,1)S(1)}, bf16[7,128,128]{2,1,0:T(8,128)(2,1)S(1)}, u32[]{:S(2)}, u32[]{:S(2)}) %collective-permute-start) | collective-permute-done | bytes 229408 | tf_op jit(solution)/shard_map/ppermute | solution.py:428
  17.9 3.1 collective-permute-start.2
  21.9 4.5 %collective-permute-done.2 = bf16[14,128,128]{2,1,0:T(8,128)(2,1)S(1)} collective-permute-done((bf16[14,128,128]{2,1,0:T(8,128)(2,1)S(1)}, bf16[14,128,128]{2,1,0:T(8,128)(2,1)S(1)}, u32[]{:S(2)}, u32[]{:S(2)}) %collective-permute-start.2) | collective-permute-done | bytes 458784 | tf_op jit(solution)/shard_map/ppermute | solution.py:428
  26.4 3.2 collective-permute-start.4
  32.5 4.5 %collective-permute-done.3 = bf16[7,128,128]{2,1,0:T(8,128)(2,1)S(1)} collective-permute-done((bf16[7,128,128]{2,1,0:T(8,128)(2,1)S(1)}, bf16[7,128,128]{2,1,0:T(8,128)(2,1)S(1)}, u32[]{:S(2)}, u32[]{:S(2)}) %collective-permute-start.3) | collective-permute-done | bytes 229408 | tf_op jit(solution)/shard_map/ppermute | solution.py:428
  38.8 2.8 collective-permute-start.5
  43.8 30.5 %collective-permute-done.5 = bf16[56,128,128]{2,1,0:T(8,128)(2,1)S(1)} collective-permute-done((bf16[56,128,128]{2,1,0:T(8,128)(2,1)S(1)}, bf16[56,128,128]{2,1,0:T(8,128)(2,1)S(1)}, u32[]{:S(2)}, u32[]{:S(2)}) %collective-permute-start.5) | collective-permute-done | bytes 1835040 | tf_op jit(solution)/shard_map/ppermute | solution.py:428
  77.1 2.8 constant_dynamic-update-slice_fusion.6
  82.9 7.1 %all-to-all-start = ((bf16[64,4,768]{2,1,0:T(4,128)(2,1)}), bf16[64,4,768]{2,1,0:T(4,128)(2,1)S(1)}, u32[]{:S(2)}, u32[]{:S(2)}) async-start(bf16[64,4,768]{2,1,0:T(4,128)(2,1)} %bitcast.4), calls=%async_computation | async-start | bytes 786432 | tf_op jit(solution)/shard_map/all_to_all | solution.py:742
  90.7 16.3 %all-to-all-done = bf16[64,4,768]{2,1,0:T(4,128)(2,1)S(1)} async-done(((bf16[64,4,768]{2,1,0:T(4,128)(2,1)}), bf16[64,4,768]{2,1,0:T(4,128)(2,1)S(1)}, u32[]{:S(2)}, u32[]{:S(2)}) %all-to-all-start) | async-done | bytes 393248 | tf_op jit(solution)/shard_map/all_to_all | solution.py:742
  111.2 3.0 constant_dynamic-update-slice_fusion.16
  114.2 7.4 %constant_dynamic-update-slice_fusion.15 = bf16[448,128,128]{2,1,0:T(8,128)(2,1)} fusion(bf16[448,128,128]{2,1,0:T(8,128)(2,1)} %constant_dynamic-update-slice_fusion.16, bf16[168,128,128]{2,1,0:T(8,128)(2,1)} %collective-permute-done.9), kind=kLoop, calls=%fused_computation.19 | loop fusion | bytes 11010048
  123.0 14.5 %first_forward.1 = (f32[256,768]{1,0:T(8,128)}, bf16[256,768]{1,0:T(8,128)(2,1)}, bf16[9,256,256]{2,1,0:T(8,128)(2,1)}, bf16[12,256,256]{2,1,0:T(8,128)(2,1)}, b...) custom-call(s32[864]{0:T(1024)} %get-tuple-element.169.refs_2_.where_ref, ...), custom_call_target="tpu_custom_call" | custom-call | tf_op jit(solution)/shard_map/first_forward/pallas_call | solution.py:370
  139.4 5.3 %all-to-all-start.1 = ((bf16[64,4,768]{2,1,0:T(4,128)(2,1)}), bf16[64,4,768]{2,1,0:T(4,128)(2,1)S(1)}, u32[]{:S(2)}, u32[]{:S(2)}) async-start(bf16[64,4,768]{2,1,0:T(4,128)(2,1)} %reshape.53), calls=%async_computation.1 | async-start | bytes 786432 | tf_op jit(solution)/shard_map/all_to_all | solution.py:742
  146.2 11.1 %all-to-all-done.1 = bf16[64,4,768]{2,1,0:T(4,128)(2,1)S(1)} async-done(((bf16[64,4,768]{2,1,0:T(4,128)(2,1)}), bf16[64,4,768]{2,1,0:T(4,128)(2,1)S(1)}, u32[]{:S(2)}, u32[]{:S(2)}) %all-to-all-start.1) | async-done | bytes 393248 | tf_op jit(solution)/shard_map/all_to_all | solution.py:742
  158.1 28.3 %second_layer.1 = (bf16[256,768]{1,0:T(8,128)(2,1)}, bf16[256,768]{1,0:T(8,128)(2,1)}, bf16[140,128,128]{2,1,0:T(8,128)(2,1)}, bf16[112,128,128]{2,1,0:T(8,128)(...) custom-call(s32[864]{0:T(1024)} %get-tuple-element.169.refs_2_.where, ...), custom_call_target="tpu_custom_call" | custom-call | tf_op jit(solution)/shard_map/second_layer/pallas_call | solution.py:383
  187.5 17.0 %all_to_all.20 = bf16[64,4,768]{2,1,0:T(4,128)(2,1)S(1)} all-to-all(bf16[64,4,768]{2,1,0:T(4,128)(2,1)S(1)} %reshape.57), channel_id=1, replica_groups=mesh['pos_0'=4,'pos_1'=2,'pos_2'=4,'pos_3'=2,'frame'=2] {'pos_0','pos_1'..., dimensions={0} | all-to-all | bytes 786432 | tf_op jit(solution)/shard_map/all_to_all | solution.py:742
  205.4 23.6 %first_backward.1 = (bf16[256,768]{1,0:T(8,128)(2,1)}, bf16[140,128,128]{2,1,0:T(8,128)(2,1)}, bf16[112,128,128]{2,1,0:T(8,128)(2,1)}, bf16[196,128,128]{2,1,0:T...) custom-call(s32[864]{0:T(1024)} %get-tuple-element.169.refs_2_.where, ...), custom_call_target="tpu_custom_call", output_to_operand_aliasing={{1}: (14, {}), {2}: (15, {}), {3}: (16, {}), {4}: (17, {}),... | custom-call | tf_op jit(solution)/shard_map/first_backward/pallas_call | solution.py:399
  229.5 7.6 %collective-permute-done.11.refs_1_ = bf16[140,128,128]{2,1,0:T(8,128)(2,1)S(1)} collective-permute-done((bf16[140,128,128]{2,1,0:T(8,128)(2,1)}, bf16[140,128,128]{2,1,0:T(8,128)(2,1)S(1)}, u32[]{:S(2)}, u32[]{:S(2)}) %collective-permute-start.11) | collective-permute-done | bytes 4587552 | tf_op jit(solution)/shard_map/ppermute | solution.py:428
  247.4 11.3 %collective-permute-done.14.refs_2_ = bf16[28,128,128]{2,1,0:T(8,128)(2,1)S(1)} collective-permute-done((bf16[28,128,128]{2,1,0:T(8,128)(2,1)}, bf16[28,128,128]{2,1,0:T(8,128)(2,1)S(1)}, u32[]{:S(2)}, u32[]{:S(2)}) %collective-permute-start.14) | collective-permute-done | bytes 917536 | tf_op jit(solution)/shard_map/ppermute | solution.py:428
  265.1 3.0 add_tiles.14
  268.2 9.5 %collective-permute-done.17.refs_2_ = bf16[84,128,128]{2,1,0:T(8,128)(2,1)S(1)} collective-permute-done((bf16[84,128,128]{2,1,0:T(8,128)(2,1)}, bf16[84,128,128]{2,1,0:T(8,128)(2,1)S(1)}, u32[]{:S(2)}, u32[]{:S(2)}) %collective-permute-start.17) | collective-permute-done | bytes 2752544 | tf_op jit(solution)/shard_map/ppermute | solution.py:428
  277.6 3.2 add_tiles.15
  286.0 3.7 add_tiles.16
  290.9 3.6 add_tiles.17
  300.0 5.9 %collective-permute-done.24.refs_1_ = bf16[7,128,128]{2,1,0:T(8,128)(2,1)S(1)} collective-permute-done((bf16[7,128,128]{2,1,0:T(8,128)(2,1)S(1)}, bf16[7,128,128]{2,1,0:T(8,128)(2,1)S(1)}, u32[]{:S(2)}, u32[]{:S(2)}) %collective-permute-start.24) | collective-permute-done | bytes 229408 | tf_op jit(solution)/shard_map/ppermute | solution.py:428
  310.8 3.4 add_tiles.19
  318.7 12.2 %all-to-all-start.3 = ((bf16[64,4,768]{2,1,0:T(4,128)(2,1)}), bf16[64,4,768]{2,1,0:T(4,128)(2,1)}, u32[]{:S(2)}, u32[]{:S(2)}) async-start(bf16[64,4,768]{2,1,0:T(4,128)(2,1)} %reshape.59), calls=%async_computation.3 | async-start | bytes 786432 | tf_op jit(solution)/shard_map/all_to_all | solution.py:742
  337.6 3.2 collective-permute-done.27.refs_3_
  354.6 6.8 %precondition.2 = (f32[14,128,128]{2,1,0:T(8,128)}, f32[14,128,128]{2,1,0:T(8,128)}, f32[14,128,128]{2,1,0:T(8,128)}, f32[14,128,128]{2,1,0:T(8,128)}) custom-call(s32[15]{0:T(128)} %get-tuple-element.170.info_ref, bf16[7,128,128]{2,1,0:T(8,128)(2,1)} %copy-done.6, bf16[7,128,128]{2,1,0:T(8,128)(2,1)} %copy-done.17, f32[14,128,128]{2,1,0:T(8,128)} %refs_1_.1, ...), custom_call_target="tpu_custom_call" | custom-call | flops 704643072 | bytes 4128768 | tf_op jit(solution)/shard_map/precondition/pallas_call | solution.py:659
  369.4 6.6 %precondition.3 = (f32[14,128,128]{2,1,0:T(8,128)}, f32[14,128,128]{2,1,0:T(8,128)}, f32[14,128,128]{2,1,0:T(8,128)}, f32[14,128,128]{2,1,0:T(8,128)}) custom-call(s32[15]{0:T(128)} %get-tuple-element.171.info_ref, bf16[7,128,128]{2,1,0:T(8,128)(2,1)} %copy-done.16, ...), custom_call_target="tpu_custom_call", output_to_operand_aliasing={{0}: (7, {}), {1}: (8, {}), {2}: (9, {}), {3}: (10, {})} | custom-call | flops 704643072 | bytes 4128768 | tf_op jit(solution)/shard_map/precondition/pallas_call | solution.py:659
  (160 shorter events, 97.2 us)
Async XLA Ops:
  7.2 115.8 %all-gather.2.cloned.1.call-start = ((), (), s32[]{:S(2)}) async-start(), calls=%async_computation.4 | async-start | bytes 14909440 | tf_op jit(solution)/shard_map/all_gather | solution.py:677
  21.0 8.8 %collective-permute-start.1 = (bf16[14,128,128]{2,1,0:T(8,128)(2,1)S(1)}, bf16[14,128,128]{2,1,0:T(8,128)(2,1)S(1)}, u32[]{:S(2)}, u32[]{:S(2)}) collective-permute-start(bf16[14,128,128]{2,1,0:T(8,128)(2,1)S(1)} %pad_maximum_fusion.1), channel_id=1, source_target_pairs={{0,4},{1,5},{2,34},{3,35},{4,8},{5,9},{6,38},{7,39},{8,12},{9,13},... | collective-permute-start | bytes 1376264 | tf_op jit(solution)/shard_map/ppermute | solution.py:428
  26.4 11.4 %collective-permute-start.4 = (bf16[7,128,128]{2,1,0:T(8,128)(2,1)S(1)}, bf16[7,128,128]{2,1,0:T(8,128)(2,1)S(1)}, u32[]{:S(2)}, u32[]{:S(2)}) collective-permute-start(bf16[7,128,128]{2,1,0:T(8,128)(2,1)S(1)} %slice.27), channel_id=1, source_target_pairs={{0,12},{1,13},{2,98},{3,99},{4,0},{5,1},{6,102},{7,103},{8,4},{9,5... | collective-permute-start | bytes 688136 | tf_op jit(solution)/shard_map/ppermute | solution.py:428
  38.8 35.5 %collective-permute-start.5 = (bf16[56,128,128]{2,1,0:T(8,128)(2,1)S(1)}, bf16[56,128,128]{2,1,0:T(8,128)(2,1)S(1)}, u32[]{:S(2)}, u32[]{:S(2)}) collective-permute-start(bf16[56,128,128]{2,1,0:T(8,128)(2,1)S(1)} %get-tuple-element.161), channel_id=1, source_target_pairs={{0,32},{1,33},{2,6},{3,7},{4,36},{5,37},{6,10},{7,11},{8,40},{9,41... | collective-permute-start | bytes 5505032 | tf_op jit(solution)/shard_map/ppermute | solution.py:428
  41.6 35.5 %collective-permute-start.6 = (bf16[56,128,128]{2,1,0:T(8,128)(2,1)S(1)}, bf16[56,128,128]{2,1,0:T(8,128)(2,1)S(1)}, u32[]{:S(2)}, u32[]{:S(2)}) collective-permute-start(bf16[56,128,128]{2,1,0:T(8,128)(2,1)S(1)} %get-tuple-element.161), channel_id=1, source_target_pairs={{0,96},{1,97},{2,14},{3,15},{4,100},{5,101},{6,2},{7,3},{8,104},{9... | collective-permute-start | bytes 5505032 | tf_op jit(solution)/shard_map/ppermute | solution.py:428
  79.9 34.3 %collective-permute-start.9 = (bf16[168,128,128]{2,1,0:T(8,128)(2,1)}, bf16[168,128,128]{2,1,0:T(8,128)(2,1)}, u32[]{:S(2)}, u32[]{:S(2)}) collective-permute-start(bf16[168,128,128]{2,1,0:T(8,128)(2,1)} %get-tuple-element.144), channel_id=1, source_target_pairs={{0,2},{1,3},{2,0},{3,1},{4,6},{5,7},{6,4},{7,5},{8,10},{9,11},{10,... | collective-permute-start | bytes 16515080 | tf_op jit(solution)/shard_map/ppermute | solution.py:428
  79.9 27.9 %collective-permute-start.8 = (bf16[28,128,128]{2,1,0:T(8,128)(2,1)S(1)}, bf16[28,128,128]{2,1,0:T(8,128)(2,1)S(1)}, u32[]{:S(2)}, u32[]{:S(2)}) collective-permute-start(bf16[28,128,128]{2,1,0:T(8,128)(2,1)S(1)} %slice.29), channel_id=1, source_target_pairs={{0,96},{1,97},{2,14},{3,15},{4,100},{5,101},{6,2},{7,3},{8,104},{9... | collective-permute-start | bytes 2752520 | tf_op jit(solution)/shard_map/ppermute | solution.py:428
  82.9 24.9 %collective-permute-start.7 = (bf16[28,128,128]{2,1,0:T(8,128)(2,1)}, bf16[28,128,128]{2,1,0:T(8,128)(2,1)S(1)}, u32[]{:S(2)}, u32[]{:S(2)}) collective-permute-start(bf16[28,128,128]{2,1,0:T(8,128)(2,1)} %slice.28), channel_id=1, source_target_pairs={{0,32},{1,33},{2,6},{3,7},{4,36},{5,37},{6,10},{7,11},{8,40},{9,41... | collective-permute-start | bytes 2752520 | tf_op jit(solution)/shard_map/ppermute | solution.py:428
  82.9 24.1 %all-to-all-start = ((bf16[64,4,768]{2,1,0:T(4,128)(2,1)}), bf16[64,4,768]{2,1,0:T(4,128)(2,1)S(1)}, u32[]{:S(2)}, u32[]{:S(2)}) async-start(bf16[64,4,768]{2,1,0:T(4,128)(2,1)} %bitcast.4), calls=%async_computation | async-start | bytes 786432 | tf_op jit(solution)/shard_map/all_to_all | solution.py:742
  109.2 12.4 %collective-permute-start.10 = (bf16[56,128,128]{2,1,0:T(8,128)(2,1)}, bf16[56,128,128]{2,1,0:T(8,128)(2,1)S(1)}, u32[]{:S(2)}, u32[]{:S(2)}) collective-permute-start(bf16[56,128,128]{2,1,0:T(8,128)(2,1)} %keep.5), channel_id=1, source_target_pairs={{0,2},{1,3},{2,0},{3,1},{4,6},{5,7},{6,4},{7,5},{8,10},{9,11},{10,... | collective-permute-start | bytes 5505032 | tf_op jit(solution)/shard_map/ppermute | solution.py:428
  139.4 17.9 %all-to-all-start.1 = ((bf16[64,4,768]{2,1,0:T(4,128)(2,1)}), bf16[64,4,768]{2,1,0:T(4,128)(2,1)S(1)}, u32[]{:S(2)}, u32[]{:S(2)}) async-start(bf16[64,4,768]{2,1,0:T(4,128)(2,1)} %reshape.53), calls=%async_computation.1 | async-start | bytes 786432 | tf_op jit(solution)/shard_map/all_to_all | solution.py:742
  243.5 21.6 %collective-permute-start.12 = (bf16[196,128,128]{2,1,0:T(8,128)(2,1)}, bf16[196,128,128]{2,1,0:T(8,128)(2,1)}, u32[]{:S(2)}, u32[]{:S(2)}) collective-permute-start(bf16[196,128,128]{2,1,0:T(8,128)(2,1)} %keep.6), channel_id=1, source_target_pairs={{0,2},{1,3},{2,0},{3,1},{4,6},{5,7},{6,4},{7,5},{8,10},{9,11},{10,... | collective-permute-start | bytes 19267592 | tf_op jit(solution)/shard_map/ppermute | solution.py:428
  243.9 15.3 %collective-permute-start.13 = (bf16[112,128,128]{2,1,0:T(8,128)(2,1)}, bf16[112,128,128]{2,1,0:T(8,128)(2,1)S(1)}, u32[]{:S(2)}, u32[]{:S(2)}) collective-permute-start(bf16[112,128,128]{2,1,0:T(8,128)(2,1)} %keep.7), channel_id=1, source_target_pairs={{0,2},{1,3},{2,0},{3,1},{4,6},{5,7},{6,4},{7,5},{8,10},{9,11},{10,... | collective-permute-start | bytes 11010056 | tf_op jit(solution)/shard_map/ppermute | solution.py:428
  244.0 33.6 %collective-permute-start.17 = (bf16[84,128,128]{2,1,0:T(8,128)(2,1)}, bf16[84,128,128]{2,1,0:T(8,128)(2,1)S(1)}, u32[]{:S(2)}, u32[]{:S(2)}) collective-permute-start(bf16[84,128,128]{2,1,0:T(8,128)(2,1)} %copy-done.11), channel_id=1, source_target_pairs={{0,1},{1,0},{2,19},{3,18},{4,5},{5,4},{6,23},{7,22},{8,9},{9,8},{1... | collective-permute-start | bytes 8257544 | tf_op jit(solution)/shard_map/ppermute | solution.py:428
  244.7 14.0 %collective-permute-start.14 = (bf16[28,128,128]{2,1,0:T(8,128)(2,1)}, bf16[28,128,128]{2,1,0:T(8,128)(2,1)S(1)}, u32[]{:S(2)}, u32[]{:S(2)}) collective-permute-start(bf16[28,128,128]{2,1,0:T(8,128)(2,1)} %copy-done.12), channel_id=1, source_target_pairs={{0,32},{1,33},{2,6},{3,7},{4,36},{5,37},{6,10},{7,11},{8,40},{9,41... | collective-permute-start | bytes 2752520 | tf_op jit(solution)/shard_map/ppermute | solution.py:428
  245.1 13.6 %collective-permute-start.15 = (bf16[28,128,128]{2,1,0:T(8,128)(2,1)S(1)}, bf16[28,128,128]{2,1,0:T(8,128)(2,1)S(1)}, u32[]{:S(2)}, u32[]{:S(2)}) collective-permute-start(bf16[28,128,128]{2,1,0:T(8,128)(2,1)S(1)} %get-tuple-element.99), channel_id=1, source_target_pairs={{0,96},{1,97},{2,14},{3,15},{4,100},{5,101},{6,2},{7,3},{8,104},{9... | collective-permute-start | bytes 2752520 | tf_op jit(solution)/shard_map/ppermute | solution.py:428
  262.3 23.6 %collective-permute-start.20 = (bf16[56,128,128]{2,1,0:T(8,128)(2,1)S(1)}, bf16[56,128,128]{2,1,0:T(8,128)(2,1)S(1)}, u32[]{:S(2)}, u32[]{:S(2)}) collective-permute-start(bf16[56,128,128]{2,1,0:T(8,128)(2,1)S(1)} %get-tuple-element.106), channel_id=1, source_target_pairs={{0,32},{1,33},{2,6},{3,7},{4,36},{5,37},{6,10},{7,11},{8,40},{9,41... | collective-permute-start | bytes 5505032 | tf_op jit(solution)/shard_map/ppermute | solution.py:428
  262.8 23.2 %collective-permute-start.21 = (bf16[56,128,128]{2,1,0:T(8,128)(2,1)S(1)}, bf16[56,128,128]{2,1,0:T(8,128)(2,1)S(1)}, u32[]{:S(2)}, u32[]{:S(2)}) collective-permute-start(bf16[56,128,128]{2,1,0:T(8,128)(2,1)S(1)} %get-tuple-element.107), channel_id=1, source_target_pairs={{0,96},{1,97},{2,14},{3,15},{4,100},{5,101},{6,2},{7,3},{8,104},{9... | collective-permute-start | bytes 5505032 | tf_op jit(solution)/shard_map/ppermute | solution.py:428
  280.8 10.1 %collective-permute-start.18 = (bf16[14,128,128]{2,1,0:T(8,128)(2,1)S(1)}, bf16[14,128,128]{2,1,0:T(8,128)(2,1)S(1)}, u32[]{:S(2)}, u32[]{:S(2)}) collective-permute-start(bf16[14,128,128]{2,1,0:T(8,128)(2,1)S(1)} %get-tuple-element.104), channel_id=1, source_target_pairs={{0,32},{1,33},{2,6},{3,7},{4,36},{5,37},{6,10},{7,11},{8,40},{9,41... | collective-permute-start | bytes 1376264 | tf_op jit(solution)/shard_map/ppermute | solution.py:428
  281.2 9.7 %collective-permute-start.19 = (bf16[14,128,128]{2,1,0:T(8,128)(2,1)S(1)}, bf16[14,128,128]{2,1,0:T(8,128)(2,1)S(1)}, u32[]{:S(2)}, u32[]{:S(2)}) collective-permute-start(bf16[14,128,128]{2,1,0:T(8,128)(2,1)S(1)} %get-tuple-element.105), channel_id=1, source_target_pairs={{0,96},{1,97},{2,14},{3,15},{4,100},{5,101},{6,2},{7,3},{8,104},{9... | collective-permute-start | bytes 1376264 | tf_op jit(solution)/shard_map/ppermute | solution.py:428
  283.5 26.1 %collective-permute-start.16 = (bf16[28,128,128]{2,1,0:T(8,128)(2,1)S(1)}, bf16[28,128,128]{2,1,0:T(8,128)(2,1)S(1)}, u32[]{:S(2)}, u32[]{:S(2)}) collective-permute-start(bf16[28,128,128]{2,1,0:T(8,128)(2,1)S(1)} %get-tuple-element.101), channel_id=1, source_target_pairs={{0,1},{1,0},{2,19},{3,18},{4,5},{5,4},{6,23},{7,22},{8,9},{9,8},{1... | collective-permute-start | bytes 2752520 | tf_op jit(solution)/shard_map/ppermute | solution.py:428
  294.5 16.3 %collective-permute-start.22 = (bf16[28,128,128]{2,1,0:T(8,128)(2,1)S(1)}, bf16[28,128,128]{2,1,0:T(8,128)(2,1)S(1)}, u32[]{:S(2)}, u32[]{:S(2)}) collective-permute-start(bf16[28,128,128]{2,1,0:T(8,128)(2,1)S(1)} %get-tuple-element.110), channel_id=1, source_target_pairs={{0,32},{1,33},{2,6},{3,7},{4,36},{5,37},{6,10},{7,11},{8,40},{9,41... | collective-permute-start | bytes 2752520 | tf_op jit(solution)/shard_map/ppermute | solution.py:428
  294.6 16.2 %collective-permute-start.23 = (bf16[28,128,128]{2,1,0:T(8,128)(2,1)S(1)}, bf16[28,128,128]{2,1,0:T(8,128)(2,1)S(1)}, u32[]{:S(2)}, u32[]{:S(2)}) collective-permute-start(bf16[28,128,128]{2,1,0:T(8,128)(2,1)S(1)} %get-tuple-element.111), channel_id=1, source_target_pairs={{0,96},{1,97},{2,14},{3,15},{4,100},{5,101},{6,2},{7,3},{8,104},{9... | collective-permute-start | bytes 2752520 | tf_op jit(solution)/shard_map/ppermute | solution.py:428
  297.3 8.6 %collective-permute-start.24 = (bf16[7,128,128]{2,1,0:T(8,128)(2,1)S(1)}, bf16[7,128,128]{2,1,0:T(8,128)(2,1)S(1)}, u32[]{:S(2)}, u32[]{:S(2)}) collective-permute-start(bf16[7,128,128]{2,1,0:T(8,128)(2,1)S(1)} %get-tuple-element.113), channel_id=1, source_target_pairs={{0,4},{1,5},{2,34},{3,35},{4,8},{5,9},{6,38},{7,39},{8,12},{9,13},... | collective-permute-start | bytes 688136 | tf_op jit(solution)/shard_map/ppermute | solution.py:428
  307.0 25.6 %collective-permute-start.28 = (bf16[14,128,128]{2,1,0:T(8,128)(2,1)}, bf16[14,128,128]{2,1,0:T(8,128)(2,1)S(1)}, u32[]{:S(2)}, u32[]{:S(2)}) collective-permute-start(bf16[14,128,128]{2,1,0:T(8,128)(2,1)} %get-tuple-element.125), channel_id=1, source_target_pairs={{0,4},{1,5},{2,34},{3,35},{4,8},{5,9},{6,38},{7,39},{8,12},{9,13},... | collective-permute-start | bytes 1376264 | tf_op jit(solution)/shard_map/ppermute | solution.py:428
  307.0 25.6 %collective-permute-start.29 = (bf16[14,128,128]{2,1,0:T(8,128)(2,1)}, bf16[14,128,128]{2,1,0:T(8,128)(2,1)}, u32[]{:S(2)}, u32[]{:S(2)}) collective-permute-start(bf16[14,128,128]{2,1,0:T(8,128)(2,1)} %get-tuple-element.126), channel_id=1, source_target_pairs={{0,12},{1,13},{2,98},{3,99},{4,0},{5,1},{6,102},{7,103},{8,4},{9,5... | collective-permute-start | bytes 1376264 | tf_op jit(solution)/shard_map/ppermute | solution.py:428
  318.7 27.3 %all-to-all-start.3 = ((bf16[64,4,768]{2,1,0:T(4,128)(2,1)}), bf16[64,4,768]{2,1,0:T(4,128)(2,1)}, u32[]{:S(2)}, u32[]{:S(2)}) async-start(bf16[64,4,768]{2,1,0:T(4,128)(2,1)} %reshape.59), calls=%async_computation.3 | async-start | bytes 786432 | tf_op jit(solution)/shard_map/all_to_all | solution.py:742
  330.9 9.9 %collective-permute-start.26 = (bf16[4,128,128]{2,1,0:T(8,128)(2,1)S(1)}, bf16[4,128,128]{2,1,0:T(8,128)(2,1)S(1)}, u32[]{:S(2)}, u32[]{:S(2)}) collective-permute-start(bf16[4,128,128]{2,1,0:T(8,128)(2,1)S(1)} %get-tuple-element.121), channel_id=1, source_target_pairs={{0,4},{1,5},{2,34},{3,35},{4,8},{5,9},{6,38},{7,39},{8,12},{9,13},... | collective-permute-start | bytes 393224 | tf_op jit(solution)/shard_map/ppermute | solution.py:428
  334.5 11.0 %collective-permute-start.32 = (bf16[7,128,128]{2,1,0:T(8,128)(2,1)S(1)}, bf16[7,128,128]{2,1,0:T(8,128)(2,1)S(1)}, u32[]{:S(2)}, u32[]{:S(2)}) collective-permute-start(bf16[7,128,128]{2,1,0:T(8,128)(2,1)S(1)} %get-tuple-element.131), channel_id=1, source_target_pairs={{0,17},{1,16},{2,19},{3,18},{4,21},{5,20},{6,23},{7,22},{8,25},{9,... | collective-permute-start | bytes 688136 | tf_op jit(solution)/shard_map/ppermute | solution.py:428
  350.2 11.2 %collective-permute-start.35 = (bf16[7,128,128]{2,1,0:T(8,128)(2,1)S(1)}, bf16[7,128,128]{2,1,0:T(8,128)(2,1)S(1)}, u32[]{:S(2)}, u32[]{:S(2)}) collective-permute-start(bf16[7,128,128]{2,1,0:T(8,128)(2,1)S(1)} %get-tuple-element.134), channel_id=1, source_target_pairs={{0,17},{1,16},{2,3},{3,2},{4,21},{5,20},{6,7},{7,6},{8,25},{9,24},... | collective-permute-start | bytes 688136 | tf_op jit(solution)/shard_map/ppermute | solution.py:428
  350.2 11.1 %collective-permute-start.34 = (bf16[7,128,128]{2,1,0:T(8,128)(2,1)S(1)}, bf16[7,128,128]{2,1,0:T(8,128)(2,1)S(1)}, u32[]{:S(2)}, u32[]{:S(2)}) collective-permute-start(bf16[7,128,128]{2,1,0:T(8,128)(2,1)S(1)} %get-tuple-element.134), channel_id=1, source_target_pairs={{0,16},{1,17},{2,18},{3,19},{4,20},{5,21},{6,22},{7,23},{8,24},{9,... | collective-permute-start | bytes 688136 | tf_op jit(solution)/shard_map/ppermute | solution.py:428
  352.2 11.7 %collective-permute-start.33 = (bf16[7,128,128]{2,1,0:T(8,128)(2,1)S(1)}, bf16[7,128,128]{2,1,0:T(8,128)(2,1)S(1)}, u32[]{:S(2)}, u32[]{:S(2)}) collective-permute-start(bf16[7,128,128]{2,1,0:T(8,128)(2,1)S(1)} %get-tuple-element.134), channel_id=1, source_target_pairs={{0,1},{1,0},{2,3},{3,2},{4,5},{5,4},{6,7},{7,6},{8,9},{9,8},{10,11... | collective-permute-start | bytes 688136 | tf_op jit(solution)/shard_map/ppermute | solution.py:428
  (32 other events, 224.1 us)
Sparse Core Ops, SparseCore 0:
  11.8 109.2 all-gather.1

commit v2 on v1

--- a/solution.py
+++ b/solution.py
@@ -595,7 +595,6 @@
         mine, got, x0, h1, h3,
     )
     h_ahead, h_behind = permute(h[0], along(1, 1)), permute(h[1], along(1, -1))
-    token_blocks = send_tokens(then(token_blocks, *add.last))
     p = add([alone(7, (0, n), (1, n), (2, n)) for n in (0, 7)], p[2], up, down)
     far = permute(p[1], across)
     sides = add(
@@ -608,7 +607,8 @@
     h_up, h_down = permute(sides[0], along(1, 1)), permute(sides[1], along(1, -1))
     (p,) = add([alone(7, (0, 0), (1, 0))], p[0], far)
     match = permute(p, twin)
-    (h,) = add([alone(7, (0, 0), (1, 0), (2, 0))], h[2], h_up, h_down, after=[token_blocks])
+    (h,) = add([alone(7, (0, 0), (1, 0), (2, 0))], h[2], h_up, h_down)
+    token_blocks = send_tokens(then(token_blocks, *add.last))
     beyond, beside, around = permute(h, pair_last), permute(h, twin), permute(h, opposite)
     told = (core == 0) & (frame == 1)
     h = added(jnp.where(told, beside, h), jnp.where(told, around, beyond))

time: 392 us -> 386 us (0.985)
  local copies, waits for them, and re-layouts: 52.6 us -> 44.9 us
    unnamed x55 -> x45, local copies, waits for them, and re-layouts: 36.1 us -> 30.5 us
  transfers between devices with their start and end apart: 42 -> 42, of which waited for: 19 -> 18; matrix products, arithmetic and copies ran while one was open for 9% -> 9% of each run, Pallas kernels for 7% -> 7%
where the time goes in v2:
time: 386 us; the launch traced here: 380 us
  waiting for transfers between devices  122 us (32%)
  Pallas kernels  99.8 us (26%)
  starting transfers between devices  74.9 us (19%)
  local copies, waits for them, and re-layouts  44.9 us (12%)
  blocking collectives  17 us (4%)
  between operations  14.9 us (4%)
  other arithmetic  6.19 us (2%)
    ppermute x38, waiting for transfers between devices, permute(): lax.ppermute(value, EVERY, [(number(*d), number(*target(*d))) for d in ev...  91.7 us
    ppermute x38, starting transfers between devices, permute(): lax.ppermute(value, EVERY, [(number(*d), number(*target(*d))) for d in ev...  47.8 us
    unnamed x45, local copies, waits for them, and re-layouts  30.5 us
    all_to_all x3, waiting for transfers between devices, to_frames(): lax.all_to_all(value.reshape(64, 4, D), POS, 0, 0, tiled=True)  30.4 us
    pallas_call x1, Pallas kernels, run_second(): pl.pallas_call(second_layer, name='second_layer', out_shape=[jax.ShapeDty...  28.3 us
    all_to_all x3, starting transfers between devices, to_frames(): lax.all_to_all(value.reshape(64, 4, D), POS, 0, 0, tiled=True)  27.1 us
    pallas_call x1, Pallas kernels, run_first_backward(): pl.pallas_call(first_backward, name='first_backward', out_shape=[jax.Shap...  23.8 us
    pallas_call x12, Pallas kernels, __call__(): pl.pallas_call(functools.partial(add_tiles, plan, len(sources), len(last)...  19.8 us
  transfers between devices with their start and end apart: 42, of which 18 were waited for; matrix products, arithmetic and copies ran while one was open for 9% of the time, Pallas kernels for 7%

profile of v2, /device:TPU:1, one launch (start us, length us, event | category | flops | bytes accessed | tf_op | source)
XLA Modules:
  0.0 379.8 jit_solution(11256701163741935364)
XLA Ops:
  9.5 3.4 collective-permute-start
  12.9 4.9 %collective-permute-done = bf16[7,128,128]{2,1,0:T(8,128)(2,1)S(1)} collective-permute-done((bf16[7,128,128]{2,1,0:T(8,128)(2,1)S(1)}, bf16[7,128,128]{2,1,0:T(8,128)(2,1)S(1)}, u32[]{:S(2)}, u32[]{:S(2)}) %collective-permute-start) | collective-permute-done | bytes 229408 | tf_op jit(solution)/shard_map/ppermute | solution.py:428
  17.9 3.1 collective-permute-start.2
  21.9 4.5 %collective-permute-done.2 = bf16[14,128,128]{2,1,0:T(8,128)(2,1)S(1)} collective-permute-done((bf16[14,128,128]{2,1,0:T(8,128)(2,1)S(1)}, bf16[14,128,128]{2,1,0:T(8,128)(2,1)S(1)}, u32[]{:S(2)}, u32[]{:S(2)}) %collective-permute-start.2) | collective-permute-done | bytes 458784 | tf_op jit(solution)/shard_map/ppermute | solution.py:428
  26.4 3.2 collective-permute-start.4
  32.5 4.4 %collective-permute-done.3 = bf16[7,128,128]{2,1,0:T(8,128)(2,1)S(1)} collective-permute-done((bf16[7,128,128]{2,1,0:T(8,128)(2,1)S(1)}, bf16[7,128,128]{2,1,0:T(8,128)(2,1)S(1)}, u32[]{:S(2)}, u32[]{:S(2)}) %collective-permute-start.3) | collective-permute-done | bytes 229408 | tf_op jit(solution)/shard_map/ppermute | solution.py:428
  43.8 30.5 %collective-permute-done.5 = bf16[56,128,128]{2,1,0:T(8,128)(2,1)S(1)} collective-permute-done((bf16[56,128,128]{2,1,0:T(8,128)(2,1)S(1)}, bf16[56,128,128]{2,1,0:T(8,128)(2,1)S(1)}, u32[]{:S(2)}, u32[]{:S(2)}) %collective-permute-start.5) | collective-permute-done | bytes 1835040 | tf_op jit(solution)/shard_map/ppermute | solution.py:428
  82.8 7.1 %all-to-all-start = ((bf16[64,4,768]{2,1,0:T(4,128)(2,1)}), bf16[64,4,768]{2,1,0:T(4,128)(2,1)S(1)}, u32[]{:S(2)}, u32[]{:S(2)}) async-start(bf16[64,4,768]{2,1,0:T(4,128)(2,1)} %bitcast.4), calls=%async_computation | async-start | bytes 786432 | tf_op jit(solution)/shard_map/all_to_all | solution.py:742
  90.7 16.3 %all-to-all-done = bf16[64,4,768]{2,1,0:T(4,128)(2,1)S(1)} async-done(((bf16[64,4,768]{2,1,0:T(4,128)(2,1)}), bf16[64,4,768]{2,1,0:T(4,128)(2,1)S(1)}, u32[]{:S(2)}, u32[]{:S(2)}) %all-to-all-start) | async-done | bytes 393248 | tf_op jit(solution)/shard_map/all_to_all | solution.py:742
  114.1 7.4 %constant_dynamic-update-slice_fusion.15 = bf16[448,128,128]{2,1,0:T(8,128)(2,1)} fusion(bf16[448,128,128]{2,1,0:T(8,128)(2,1)} %constant_dynamic-update-slice_fusion.16, bf16[168,128,128]{2,1,0:T(8,128)(2,1)} %collective-permute-done.9), kind=kLoop, calls=%fused_computation.19 | loop fusion | bytes 11010048
  123.0 14.5 %first_forward.1 = (f32[256,768]{1,0:T(8,128)}, bf16[256,768]{1,0:T(8,128)(2,1)}, bf16[9,256,256]{2,1,0:T(8,128)(2,1)}, bf16[12,256,256]{2,1,0:T(8,128)(2,1)}, b...) custom-call(s32[864]{0:T(1024)} %get-tuple-element.171.refs_2_.where_ref, ...), custom_call_target="tpu_custom_call" | custom-call | tf_op jit(solution)/shard_map/first_forward/pallas_call | solution.py:370
  139.4 5.2 %all-to-all-start.1 = ((bf16[64,4,768]{2,1,0:T(4,128)(2,1)}), bf16[64,4,768]{2,1,0:T(4,128)(2,1)S(1)}, u32[]{:S(2)}, u32[]{:S(2)}) async-start(bf16[64,4,768]{2,1,0:T(4,128)(2,1)} %reshape.50), calls=%async_computation.1 | async-start | bytes 786432 | tf_op jit(solution)/shard_map/all_to_all | solution.py:742
  146.2 11.1 %all-to-all-done.1 = bf16[64,4,768]{2,1,0:T(4,128)(2,1)S(1)} async-done(((bf16[64,4,768]{2,1,0:T(4,128)(2,1)}), bf16[64,4,768]{2,1,0:T(4,128)(2,1)S(1)}, u32[]{:S(2)}, u32[]{:S(2)}) %all-to-all-start.1) | async-done | bytes 393248 | tf_op jit(solution)/shard_map/all_to_all | solution.py:742
  158.1 28.3 %second_layer.1 = (bf16[256,768]{1,0:T(8,128)(2,1)}, bf16[256,768]{1,0:T(8,128)(2,1)}, bf16[140,128,128]{2,1,0:T(8,128)(2,1)}, bf16[112,128,128]{2,1,0:T(8,128)(...) custom-call(s32[864]{0:T(1024)} %get-tuple-element.171.refs_2_.where, ...), custom_call_target="tpu_custom_call" | custom-call | tf_op jit(solution)/shard_map/second_layer/pallas_call | solution.py:383
  187.5 17.0 %all_to_all.20 = bf16[64,4,768]{2,1,0:T(4,128)(2,1)S(1)} all-to-all(bf16[64,4,768]{2,1,0:T(4,128)(2,1)S(1)} %reshape.54), channel_id=1, replica_groups=mesh['pos_0'=4,'pos_1'=2,'pos_2'=4,'pos_3'=2,'frame'=2] {'pos_0','pos_1'..., dimensions={0} | all-to-all | bytes 786432 | tf_op jit(solution)/shard_map/all_to_all | solution.py:742
  205.4 23.8 %first_backward.1 = (bf16[256,768]{1,0:T(8,128)(2,1)}, bf16[140,128,128]{2,1,0:T(8,128)(2,1)}, bf16[112,128,128]{2,1,0:T(8,128)(2,1)}, bf16[196,128,128]{2,1,0:T...) custom-call(s32[864]{0:T(1024)} %get-tuple-element.171.refs_2_.where, ...), custom_call_target="tpu_custom_call", output_to_operand_aliasing={{1}: (14, {}), {2}: (15, {}), {3}: (16, {}), {4}: (17, {}),... | custom-call | tf_op jit(solution)/shard_map/first_backward/pallas_call | solution.py:399
  229.5 7.7 %collective-permute-done.11.refs_1_ = bf16[140,128,128]{2,1,0:T(8,128)(2,1)S(1)} collective-permute-done((bf16[140,128,128]{2,1,0:T(8,128)(2,1)}, bf16[140,128,128]{2,1,0:T(8,128)(2,1)S(1)}, u32[]{:S(2)}, u32[]{:S(2)}) %collective-permute-start.11) | collective-permute-done | bytes 4587552 | tf_op jit(solution)/shard_map/ppermute | solution.py:428
  247.5 11.3 %collective-permute-done.14.refs_2_ = bf16[28,128,128]{2,1,0:T(8,128)(2,1)S(1)} collective-permute-done((bf16[28,128,128]{2,1,0:T(8,128)(2,1)}, bf16[28,128,128]{2,1,0:T(8,128)(2,1)S(1)}, u32[]{:S(2)}, u32[]{:S(2)}) %collective-permute-start.14) | collective-permute-done | bytes 917536 | tf_op jit(solution)/shard_map/ppermute | solution.py:428
  264.7 3.0 add_tiles.14
  267.8 10.1 %collective-permute-done.17.refs_2_ = bf16[84,128,128]{2,1,0:T(8,128)(2,1)S(1)} collective-permute-done((bf16[84,128,128]{2,1,0:T(8,128)(2,1)}, bf16[84,128,128]{2,1,0:T(8,128)(2,1)S(1)}, u32[]{:S(2)}, u32[]{:S(2)}) %collective-permute-start.17) | collective-permute-done | bytes 2752544 | tf_op jit(solution)/shard_map/ppermute | solution.py:428
  277.8 3.2 add_tiles.15
  285.6 3.7 add_tiles.16
  290.5 3.6 add_tiles.17
  299.7 5.6 %collective-permute-done.24.refs_1_ = bf16[7,128,128]{2,1,0:T(8,128)(2,1)S(1)} collective-permute-done((bf16[7,128,128]{2,1,0:T(8,128)(2,1)S(1)}, bf16[7,128,128]{2,1,0:T(8,128)(2,1)S(1)}, u32[]{:S(2)}, u32[]{:S(2)}) %collective-permute-start.24) | collective-permute-done | bytes 229408 | tf_op jit(solution)/shard_map/ppermute | solution.py:428
  310.4 3.4 add_tiles.19
  314.2 3.9 %collective-permute-done.28.refs_1_ = bf16[14,128,128]{2,1,0:T(8,128)(2,1)S(1)} collective-permute-done((bf16[14,128,128]{2,1,0:T(8,128)(2,1)S(1)}, bf16[14,128,128]{2,1,0:T(8,128)(2,1)S(1)}, u32[]{:S(2)}, u32[]{:S(2)}) %collective-permute-start.28) | collective-permute-done | bytes 458784 | tf_op jit(solution)/shard_map/ppermute | solution.py:428
  323.2 3.1 collective-permute-start.31
  331.2 3.2 collective-permute-start.34
  337.1 14.7 %all-to-all-start.3 = ((bf16[64,4,768]{2,1,0:T(4,128)(2,1)}), bf16[64,4,768]{2,1,0:T(4,128)(2,1)S(1)}, u32[]{:S(2)}, u32[]{:S(2)}) async-start(bf16[64,4,768]{2,1,0:T(4,128)(2,1)} %reshape.56), calls=%async_computation.3 | async-start | bytes 786432 | tf_op jit(solution)/shard_map/all_to_all | solution.py:742
  352.5 6.8 %precondition.2 = (f32[14,128,128]{2,1,0:T(8,128)}, f32[14,128,128]{2,1,0:T(8,128)}, f32[14,128,128]{2,1,0:T(8,128)}, f32[14,128,128]{2,1,0:T(8,128)}) custom-call(s32[15]{0:T(128)} %get-tuple-element.172.info_ref, bf16[7,128,128]{2,1,0:T(8,128)(2,1)} %copy-done.2, bf16[7,128,128]{2,1,0:T(8,128)(2,1)} %copy-done.12, f32[14,128,128]{2,1,0:T(8,128)} %refs_1_.1, ...), custom_call_target="tpu_custom_call" | custom-call | flops 704643072 | bytes 4128768 | tf_op jit(solution)/shard_map/precondition/pallas_call | solution.py:659
  361.4 3.0 all-to-all-done.3
  365.1 6.6 %precondition.3 = (f32[14,128,128]{2,1,0:T(8,128)}, f32[14,128,128]{2,1,0:T(8,128)}, f32[14,128,128]{2,1,0:T(8,128)}, f32[14,128,128]{2,1,0:T(8,128)}) custom-call(s32[15]{0:T(128)} %get-tuple-element.173.info_ref, bf16[7,128,128]{2,1,0:T(8,128)(2,1)} %copy-done.11, ...), custom_call_target="tpu_custom_call", output_to_operand_aliasing={{0}: (7, {}), {1}: (8, {}), {2}: (9, {}), {3}: (10, {})} | custom-call | flops 704643072 | bytes 4128768 | tf_op jit(solution)/shard_map/precondition/pallas_call | solution.py:659
  (149 shorter events, 87.2 us)
Async XLA Ops:
  7.2 115.9 %all-gather.2.cloned.1.call-start = ((), (), s32[]{:S(2)}) async-start(), calls=%async_computation.4 | async-start | bytes 14909440 | tf_op jit(solution)/shard_map/all_gather | solution.py:677
  17.9 8.5 %collective-permute-start.2 = (bf16[14,128,128]{2,1,0:T(8,128)(2,1)S(1)}, bf16[14,128,128]{2,1,0:T(8,128)(2,1)S(1)}, u32[]{:S(2)}, u32[]{:S(2)}) collective-permute-start(bf16[14,128,128]{2,1,0:T(8,128)(2,1)S(1)} %pad_maximum_fusion.1), channel_id=1, source_target_pairs={{0,12},{1,13},{2,98},{3,99},{4,0},{5,1},{6,102},{7,103},{8,4},{9,5... | collective-permute-start | bytes 1376264 | tf_op jit(solution)/shard_map/ppermute | solution.py:428
  21.0 8.8 %collective-permute-start.1 = (bf16[14,128,128]{2,1,0:T(8,128)(2,1)S(1)}, bf16[14,128,128]{2,1,0:T(8,128)(2,1)S(1)}, u32[]{:S(2)}, u32[]{:S(2)}) collective-permute-start(bf16[14,128,128]{2,1,0:T(8,128)(2,1)S(1)} %pad_maximum_fusion.1), channel_id=1, source_target_pairs={{0,4},{1,5},{2,34},{3,35},{4,8},{5,9},{6,38},{7,39},{8,12},{9,13},... | collective-permute-start | bytes 1376264 | tf_op jit(solution)/shard_map/ppermute | solution.py:428
  26.4 11.4 %collective-permute-start.4 = (bf16[7,128,128]{2,1,0:T(8,128)(2,1)S(1)}, bf16[7,128,128]{2,1,0:T(8,128)(2,1)S(1)}, u32[]{:S(2)}, u32[]{:S(2)}) collective-permute-start(bf16[7,128,128]{2,1,0:T(8,128)(2,1)S(1)} %slice.27), channel_id=1, source_target_pairs={{0,12},{1,13},{2,98},{3,99},{4,0},{5,1},{6,102},{7,103},{8,4},{9,5... | collective-permute-start | bytes 688136 | tf_op jit(solution)/shard_map/ppermute | solution.py:428
  38.8 35.5 %collective-permute-start.5 = (bf16[56,128,128]{2,1,0:T(8,128)(2,1)S(1)}, bf16[56,128,128]{2,1,0:T(8,128)(2,1)S(1)}, u32[]{:S(2)}, u32[]{:S(2)}) collective-permute-start(bf16[56,128,128]{2,1,0:T(8,128)(2,1)S(1)} %get-tuple-element.163), channel_id=1, source_target_pairs={{0,32},{1,33},{2,6},{3,7},{4,36},{5,37},{6,10},{7,11},{8,40},{9,41... | collective-permute-start | bytes 5505032 | tf_op jit(solution)/shard_map/ppermute | solution.py:428
  41.6 35.5 %collective-permute-start.6 = (bf16[56,128,128]{2,1,0:T(8,128)(2,1)S(1)}, bf16[56,128,128]{2,1,0:T(8,128)(2,1)S(1)}, u32[]{:S(2)}, u32[]{:S(2)}) collective-permute-start(bf16[56,128,128]{2,1,0:T(8,128)(2,1)S(1)} %get-tuple-element.163), channel_id=1, source_target_pairs={{0,96},{1,97},{2,14},{3,15},{4,100},{5,101},{6,2},{7,3},{8,104},{9... | collective-permute-start | bytes 5505032 | tf_op jit(solution)/shard_map/ppermute | solution.py:428
  79.9 34.2 %collective-permute-start.9 = (bf16[168,128,128]{2,1,0:T(8,128)(2,1)}, bf16[168,128,128]{2,1,0:T(8,128)(2,1)}, u32[]{:S(2)}, u32[]{:S(2)}) collective-permute-start(bf16[168,128,128]{2,1,0:T(8,128)(2,1)} %get-tuple-element.146), channel_id=1, source_target_pairs={{0,2},{1,3},{2,0},{3,1},{4,6},{5,7},{6,4},{7,5},{8,10},{9,11},{10,... | collective-permute-start | bytes 16515080 | tf_op jit(solution)/shard_map/ppermute | solution.py:428
  80.0 27.8 %collective-permute-start.8 = (bf16[28,128,128]{2,1,0:T(8,128)(2,1)S(1)}, bf16[28,128,128]{2,1,0:T(8,128)(2,1)S(1)}, u32[]{:S(2)}, u32[]{:S(2)}) collective-permute-start(bf16[28,128,128]{2,1,0:T(8,128)(2,1)S(1)} %slice.29), channel_id=1, source_target_pairs={{0,96},{1,97},{2,14},{3,15},{4,100},{5,101},{6,2},{7,3},{8,104},{9... | collective-permute-start | bytes 2752520 | tf_op jit(solution)/shard_map/ppermute | solution.py:428
  82.8 24.9 %collective-permute-start.7 = (bf16[28,128,128]{2,1,0:T(8,128)(2,1)}, bf16[28,128,128]{2,1,0:T(8,128)(2,1)S(1)}, u32[]{:S(2)}, u32[]{:S(2)}) collective-permute-start(bf16[28,128,128]{2,1,0:T(8,128)(2,1)} %slice.28), channel_id=1, source_target_pairs={{0,32},{1,33},{2,6},{3,7},{4,36},{5,37},{6,10},{7,11},{8,40},{9,41... | collective-permute-start | bytes 2752520 | tf_op jit(solution)/shard_map/ppermute | solution.py:428
  82.8 24.1 %all-to-all-start = ((bf16[64,4,768]{2,1,0:T(4,128)(2,1)}), bf16[64,4,768]{2,1,0:T(4,128)(2,1)S(1)}, u32[]{:S(2)}, u32[]{:S(2)}) async-start(bf16[64,4,768]{2,1,0:T(4,128)(2,1)} %bitcast.4), calls=%async_computation | async-start | bytes 786432 | tf_op jit(solution)/shard_map/all_to_all | solution.py:742
  109.2 12.4 %collective-permute-start.10 = (bf16[56,128,128]{2,1,0:T(8,128)(2,1)}, bf16[56,128,128]{2,1,0:T(8,128)(2,1)S(1)}, u32[]{:S(2)}, u32[]{:S(2)}) collective-permute-start(bf16[56,128,128]{2,1,0:T(8,128)(2,1)} %keep.5), channel_id=1, source_target_pairs={{0,2},{1,3},{2,0},{3,1},{4,6},{5,7},{6,4},{7,5},{8,10},{9,11},{10,... | collective-permute-start | bytes 5505032 | tf_op jit(solution)/shard_map/ppermute | solution.py:428
  139.4 17.9 %all-to-all-start.1 = ((bf16[64,4,768]{2,1,0:T(4,128)(2,1)}), bf16[64,4,768]{2,1,0:T(4,128)(2,1)S(1)}, u32[]{:S(2)}, u32[]{:S(2)}) async-start(bf16[64,4,768]{2,1,0:T(4,128)(2,1)} %reshape.50), calls=%async_computation.1 | async-start | bytes 786432 | tf_op jit(solution)/shard_map/all_to_all | solution.py:742
  243.7 21.0 %collective-permute-start.12 = (bf16[196,128,128]{2,1,0:T(8,128)(2,1)}, bf16[196,128,128]{2,1,0:T(8,128)(2,1)}, u32[]{:S(2)}, u32[]{:S(2)}) collective-permute-start(bf16[196,128,128]{2,1,0:T(8,128)(2,1)} %keep.6), channel_id=1, source_target_pairs={{0,2},{1,3},{2,0},{3,1},{4,6},{5,7},{6,4},{7,5},{8,10},{9,11},{10,... | collective-permute-start | bytes 19267592 | tf_op jit(solution)/shard_map/ppermute | solution.py:428
  243.9 14.9 %collective-permute-start.13 = (bf16[112,128,128]{2,1,0:T(8,128)(2,1)}, bf16[112,128,128]{2,1,0:T(8,128)(2,1)S(1)}, u32[]{:S(2)}, u32[]{:S(2)}) collective-permute-start(bf16[112,128,128]{2,1,0:T(8,128)(2,1)} %keep.7), channel_id=1, source_target_pairs={{0,2},{1,3},{2,0},{3,1},{4,6},{5,7},{6,4},{7,5},{8,10},{9,11},{10,... | collective-permute-start | bytes 11010056 | tf_op jit(solution)/shard_map/ppermute | solution.py:428
  244.2 33.6 %collective-permute-start.17 = (bf16[84,128,128]{2,1,0:T(8,128)(2,1)}, bf16[84,128,128]{2,1,0:T(8,128)(2,1)S(1)}, u32[]{:S(2)}, u32[]{:S(2)}) collective-permute-start(bf16[84,128,128]{2,1,0:T(8,128)(2,1)} %copy-done.6), channel_id=1, source_target_pairs={{0,1},{1,0},{2,19},{3,18},{4,5},{5,4},{6,23},{7,22},{8,9},{9,8},{1... | collective-permute-start | bytes 8257544 | tf_op jit(solution)/shard_map/ppermute | solution.py:428
  244.8 14.0 %collective-permute-start.14 = (bf16[28,128,128]{2,1,0:T(8,128)(2,1)}, bf16[28,128,128]{2,1,0:T(8,128)(2,1)S(1)}, u32[]{:S(2)}, u32[]{:S(2)}) collective-permute-start(bf16[28,128,128]{2,1,0:T(8,128)(2,1)} %copy-done.7), channel_id=1, source_target_pairs={{0,32},{1,33},{2,6},{3,7},{4,36},{5,37},{6,10},{7,11},{8,40},{9,41... | collective-permute-start | bytes 2752520 | tf_op jit(solution)/shard_map/ppermute | solution.py:428
  245.1 13.6 %collective-permute-start.15 = (bf16[28,128,128]{2,1,0:T(8,128)(2,1)S(1)}, bf16[28,128,128]{2,1,0:T(8,128)(2,1)S(1)}, u32[]{:S(2)}, u32[]{:S(2)}) collective-permute-start(bf16[28,128,128]{2,1,0:T(8,128)(2,1)S(1)} %get-tuple-element.100), channel_id=1, source_target_pairs={{0,96},{1,97},{2,14},{3,15},{4,100},{5,101},{6,2},{7,3},{8,104},{9... | collective-permute-start | bytes 2752520 | tf_op jit(solution)/shard_map/ppermute | solution.py:428
  262.0 23.6 %collective-permute-start.20 = (bf16[56,128,128]{2,1,0:T(8,128)(2,1)S(1)}, bf16[56,128,128]{2,1,0:T(8,128)(2,1)S(1)}, u32[]{:S(2)}, u32[]{:S(2)}) collective-permute-start(bf16[56,128,128]{2,1,0:T(8,128)(2,1)S(1)} %get-tuple-element.107), channel_id=1, source_target_pairs={{0,32},{1,33},{2,6},{3,7},{4,36},{5,37},{6,10},{7,11},{8,40},{9,41... | collective-permute-start | bytes 5505032 | tf_op jit(solution)/shard_map/ppermute | solution.py:428
  263.0 22.6 %collective-permute-start.21 = (bf16[56,128,128]{2,1,0:T(8,128)(2,1)S(1)}, bf16[56,128,128]{2,1,0:T(8,128)(2,1)S(1)}, u32[]{:S(2)}, u32[]{:S(2)}) collective-permute-start(bf16[56,128,128]{2,1,0:T(8,128)(2,1)S(1)} %get-tuple-element.108), channel_id=1, source_target_pairs={{0,96},{1,97},{2,14},{3,15},{4,100},{5,101},{6,2},{7,3},{8,104},{9... | collective-permute-start | bytes 5505032 | tf_op jit(solution)/shard_map/ppermute | solution.py:428
  281.0 9.5 %collective-permute-start.18 = (bf16[14,128,128]{2,1,0:T(8,128)(2,1)S(1)}, bf16[14,128,128]{2,1,0:T(8,128)(2,1)S(1)}, u32[]{:S(2)}, u32[]{:S(2)}) collective-permute-start(bf16[14,128,128]{2,1,0:T(8,128)(2,1)S(1)} %get-tuple-element.105), channel_id=1, source_target_pairs={{0,32},{1,33},{2,6},{3,7},{4,36},{5,37},{6,10},{7,11},{8,40},{9,41... | collective-permute-start | bytes 1376264 | tf_op jit(solution)/shard_map/ppermute | solution.py:428
  281.4 9.1 %collective-permute-start.19 = (bf16[14,128,128]{2,1,0:T(8,128)(2,1)S(1)}, bf16[14,128,128]{2,1,0:T(8,128)(2,1)S(1)}, u32[]{:S(2)}, u32[]{:S(2)}) collective-permute-start(bf16[14,128,128]{2,1,0:T(8,128)(2,1)S(1)} %get-tuple-element.106), channel_id=1, source_target_pairs={{0,96},{1,97},{2,14},{3,15},{4,100},{5,101},{6,2},{7,3},{8,104},{9... | collective-permute-start | bytes 1376264 | tf_op jit(solution)/shard_map/ppermute | solution.py:428
  283.8 24.4 %collective-permute-start.16 = (bf16[28,128,128]{2,1,0:T(8,128)(2,1)S(1)}, bf16[28,128,128]{2,1,0:T(8,128)(2,1)S(1)}, u32[]{:S(2)}, u32[]{:S(2)}) collective-permute-start(bf16[28,128,128]{2,1,0:T(8,128)(2,1)S(1)} %get-tuple-element.102), channel_id=1, source_target_pairs={{0,1},{1,0},{2,19},{3,18},{4,5},{5,4},{6,23},{7,22},{8,9},{9,8},{1... | collective-permute-start | bytes 2752520 | tf_op jit(solution)/shard_map/ppermute | solution.py:428
  294.2 16.3 %collective-permute-start.22 = (bf16[28,128,128]{2,1,0:T(8,128)(2,1)S(1)}, bf16[28,128,128]{2,1,0:T(8,128)(2,1)S(1)}, u32[]{:S(2)}, u32[]{:S(2)}) collective-permute-start(bf16[28,128,128]{2,1,0:T(8,128)(2,1)S(1)} %get-tuple-element.111), channel_id=1, source_target_pairs={{0,32},{1,33},{2,6},{3,7},{4,36},{5,37},{6,10},{7,11},{8,40},{9,41... | collective-permute-start | bytes 2752520 | tf_op jit(solution)/shard_map/ppermute | solution.py:428
  294.6 15.8 %collective-permute-start.23 = (bf16[28,128,128]{2,1,0:T(8,128)(2,1)S(1)}, bf16[28,128,128]{2,1,0:T(8,128)(2,1)S(1)}, u32[]{:S(2)}, u32[]{:S(2)}) collective-permute-start(bf16[28,128,128]{2,1,0:T(8,128)(2,1)S(1)} %get-tuple-element.112), channel_id=1, source_target_pairs={{0,96},{1,97},{2,14},{3,15},{4,100},{5,101},{6,2},{7,3},{8,104},{9... | collective-permute-start | bytes 2752520 | tf_op jit(solution)/shard_map/ppermute | solution.py:428
  305.4 12.7 %collective-permute-start.28 = (bf16[14,128,128]{2,1,0:T(8,128)(2,1)S(1)}, bf16[14,128,128]{2,1,0:T(8,128)(2,1)S(1)}, u32[]{:S(2)}, u32[]{:S(2)}) collective-permute-start(bf16[14,128,128]{2,1,0:T(8,128)(2,1)S(1)} %get-tuple-element.125), channel_id=1, source_target_pairs={{0,4},{1,5},{2,34},{3,35},{4,8},{5,9},{6,38},{7,39},{8,12},{9,13},... | collective-permute-start | bytes 1376264 | tf_op jit(solution)/shard_map/ppermute | solution.py:428
  305.5 12.6 %collective-permute-start.29 = (bf16[14,128,128]{2,1,0:T(8,128)(2,1)S(1)}, bf16[14,128,128]{2,1,0:T(8,128)(2,1)S(1)}, u32[]{:S(2)}, u32[]{:S(2)}) collective-permute-start(bf16[14,128,128]{2,1,0:T(8,128)(2,1)S(1)} %get-tuple-element.126), channel_id=1, source_target_pairs={{0,12},{1,13},{2,98},{3,99},{4,0},{5,1},{6,102},{7,103},{8,4},{9,5... | collective-permute-start | bytes 1376264 | tf_op jit(solution)/shard_map/ppermute | solution.py:428
  313.8 8.9 %collective-permute-start.26 = (bf16[4,128,128]{2,1,0:T(8,128)(2,1)S(1)}, bf16[4,128,128]{2,1,0:T(8,128)(2,1)S(1)}, u32[]{:S(2)}, u32[]{:S(2)}) collective-permute-start(bf16[4,128,128]{2,1,0:T(8,128)(2,1)S(1)} %get-tuple-element.121), channel_id=1, source_target_pairs={{0,4},{1,5},{2,34},{3,35},{4,8},{5,9},{6,38},{7,39},{8,12},{9,13},... | collective-permute-start | bytes 393224 | tf_op jit(solution)/shard_map/ppermute | solution.py:428
  326.4 25.5 %collective-permute-start.36 = (bf16[7,128,128]{2,1,0:T(8,128)(2,1)S(1)}, bf16[7,128,128]{2,1,0:T(8,128)(2,1)S(1)}, u32[]{:S(2)}, u32[]{:S(2)}) collective-permute-start(bf16[7,128,128]{2,1,0:T(8,128)(2,1)S(1)} %get-tuple-element.137.refs_0_), channel_id=1, source_target_pairs={{0,1},{1,0},{2,3},{3,2},{4,5},{5,4},{6,7},{7,6},{8,9},{9,8},{10,11... | collective-permute-start | bytes 688136 | tf_op jit(solution)/shard_map/ppermute | solution.py:428
  330.3 29.0 %collective-permute-start.35 = (bf16[7,128,128]{2,1,0:T(8,128)(2,1)S(1)}, bf16[7,128,128]{2,1,0:T(8,128)(2,1)S(1)}, u32[]{:S(2)}, u32[]{:S(2)}) collective-permute-start(bf16[7,128,128]{2,1,0:T(8,128)(2,1)S(1)} %get-tuple-element.136), channel_id=1, source_target_pairs={{0,17},{1,16},{2,3},{3,2},{4,21},{5,20},{6,7},{7,6},{8,25},{9,24},... | collective-permute-start | bytes 688136 | tf_op jit(solution)/shard_map/ppermute | solution.py:428
  331.2 28.1 %collective-permute-start.34 = (bf16[7,128,128]{2,1,0:T(8,128)(2,1)S(1)}, bf16[7,128,128]{2,1,0:T(8,128)(2,1)S(1)}, u32[]{:S(2)}, u32[]{:S(2)}) collective-permute-start(bf16[7,128,128]{2,1,0:T(8,128)(2,1)S(1)} %get-tuple-element.136), channel_id=1, source_target_pairs={{0,16},{1,17},{2,18},{3,19},{4,20},{5,21},{6,22},{7,23},{8,24},{9,... | collective-permute-start | bytes 688136 | tf_op jit(solution)/shard_map/ppermute | solution.py:428
  334.4 24.9 %collective-permute-start.33 = (bf16[7,128,128]{2,1,0:T(8,128)(2,1)S(1)}, bf16[7,128,128]{2,1,0:T(8,128)(2,1)S(1)}, u32[]{:S(2)}, u32[]{:S(2)}) collective-permute-start(bf16[7,128,128]{2,1,0:T(8,128)(2,1)S(1)} %get-tuple-element.136), channel_id=1, source_target_pairs={{0,1},{1,0},{2,3},{3,2},{4,5},{5,4},{6,7},{7,6},{8,9},{9,8},{10,11... | collective-permute-start | bytes 688136 | tf_op jit(solution)/shard_map/ppermute | solution.py:428
  337.1 27.4 %all-to-all-start.3 = ((bf16[64,4,768]{2,1,0:T(4,128)(2,1)}), bf16[64,4,768]{2,1,0:T(4,128)(2,1)S(1)}, u32[]{:S(2)}, u32[]{:S(2)}) async-start(bf16[64,4,768]{2,1,0:T(4,128)(2,1)} %reshape.56), calls=%async_computation.3 | async-start | bytes 786432 | tf_op jit(solution)/shard_map/all_to_all | solution.py:742
  (27 other events, 270.1 us)
Sparse Core Ops, SparseCore 0:
  11.8 109.2 all-gather.1
